TPU v7x, 128 devices: a whole 4x4x4 slice. The times are simulated.
128 devices in a mesh: rows: 32 (over x, y, core), grp: 4 (over z).
Axes of the slice: x: 4, y: 4, z: 4, core: 2. Of those that a mesh axis runs over, the one named last changes fastest.
Arguments:
- embeddings: bfloat16 [131072, 768], P('rows')
- partner: int32 [32, 32], P(None, 'rows'), may hold values from 0 to 15
- links: int32 [32, 32, 4], P('rows'), may hold values from 0 to 15, as said below
- counts: int32 [32, 32], P('rows'), may hold values from 0 to 4, as said below
Outputs:
- refined: bfloat16 [131072, 768], P('rows')
Inputs may be any that keep to these rules, and one draw needn't show every extreme that they name: The 4 entries of links[d, p] are different local block numbers. counts[d, d] is 0; 0 means that rows index d pairs none of its blocks with rows index p.
All inputs are finite; a program needn't handle non-finite values.
Results may differ from a plain program's by a relative error of at most 0.0038.
Values may be sent and summed in bfloat16 or wider, within the bound.
A program may use at most 192 MiB of HBM per device.

v0:
```python
import jax
import jax.numpy as jnp
from jax import lax
from jax.sharding import PartitionSpec as P

BLOCK = 256
LINKS = 4


def row_scaled(values):
    return values * lax.rsqrt(jnp.mean(values * values, axis=-1, keepdims=True) + 1e-06)


def on_device(embeddings, partner, links, counts):
    row_count = lax.axis_size("rows")
    group_count = lax.axis_size("grp")
    my_row = lax.axis_index("rows")
    my_group = lax.axis_index("grp")
    features = embeddings.shape[1]
    blk_here = embeddings.shape[0] // BLOCK
    wanted = partner[:, 0]
    my_links = links[0]
    my_counts = counts[0]
    offsets = jnp.arange(row_count, dtype=jnp.int32)
    target = (my_row + offsets) % row_count
    listed = my_counts[target] > 0
    executor_of = (offsets - 1) * group_count // (row_count - 1)
    assigned = listed & (executor_of == my_group)
    sort_key = jnp.where(assigned, offsets, offsets + row_count)
    visit_order = target[jnp.argsort(sort_key)]
    visit_count = jnp.sum(assigned.astype(jnp.int32))
    current = embeddings
    normed = row_scaled(current.astype(jnp.float32)).astype(jnp.bfloat16)
    blocks = normed.reshape(blk_here, BLOCK, features)
    outgoing = blocks[wanted]
    fetched = lax.all_to_all(outgoing, "rows", split_axis=0, concat_axis=0, tiled=True)
    groups = blocks.reshape(blk_here // group_count, group_count, BLOCK, features)
    own_group = lax.dynamic_index_in_dim(groups, my_group, 1, keepdims=False)
    cosines = (
        jnp.einsum("kad,kbd->kab", own_group, own_group, preferred_element_type=jnp.float32)
        / features
    )
    weight = (jnp.maximum(cosines, 0.0) ** 3).astype(jnp.bfloat16)
    diagonal = jnp.einsum("kab,kbd->kad", weight, own_group, preferred_element_type=jnp.float32)
    totals = jnp.zeros((blk_here // group_count, group_count, BLOCK, features), jnp.float32)
    totals = lax.dynamic_update_index_in_dim(totals, diagonal, my_group, 1)
    totals = totals.reshape(blk_here, BLOCK, features)
    returned = jnp.zeros((row_count, BLOCK, features), jnp.bfloat16)

    def visit(position, state_pair):
        totals_now, returned_now = state_pair
        peer_slot = visit_order[position]
        remote = lax.dynamic_index_in_dim(fetched, peer_slot, 0, keepdims=False)
        picked = lax.dynamic_index_in_dim(my_links, peer_slot, 0, keepdims=False)
        own_blocks = blocks[picked]
        pair_cosines = (
            jnp.einsum("kad,bd->kab", own_blocks, remote, preferred_element_type=jnp.float32)
            / features
        )
        active = (jnp.arange(LINKS) < my_counts[peer_slot])[:, None, None]
        pair_weight = jnp.where(active, jnp.maximum(pair_cosines, 0.0) ** 3, 0.0).astype(
            jnp.bfloat16
        )
        forward = jnp.einsum("kab,bd->kad", pair_weight, remote, preferred_element_type=jnp.float32)
        totals_now = totals_now.at[picked].add(forward)
        returned_term = jnp.einsum(
            "kab,kad->bd", pair_weight, own_blocks, preferred_element_type=jnp.float32
        ).astype(jnp.bfloat16)
        returned_now = lax.dynamic_update_index_in_dim(returned_now, returned_term, peer_slot, 0)
        return (totals_now, returned_now)

    totals, returned = lax.fori_loop(0, visit_count, visit, (totals, returned))
    came_back = lax.all_to_all(returned, "rows", split_axis=0, concat_axis=0, tiled=True)
    totals = totals.at[wanted].add(came_back.astype(jnp.float32))
    summed = lax.psum(totals, "grp")
    current = row_scaled(summed).astype(jnp.bfloat16).reshape(blk_here * BLOCK, features)
    return current


def solution(mesh):
    placed = (P("rows", None), P(None, "rows"), P("rows", None, None), P("rows", None))
    return jax.shard_map(
        on_device, mesh=mesh, in_specs=placed, out_specs=P("rows", None), check_vma=False
    )
```

profile of v0, /device:TPU:14, one launch (start us, length us, event | category | flops | bytes accessed | tf_op | source)
XLA Modules:
  0.0 859.9 jit_solution(6195599441105383110)
XLA Ops:
  7.2 4.1 fusion.15
  11.3 7.3 fusion.16
  18.6 9.5 %gather_fusion.3 = bf16[32,256,768]{2,1,0:T(8,128)(2,1)} fusion(bf16[16,256,768]{2,1,0:T(8,128)(2,1)} %bitcast.84, s32[1024]{0:T(1024)S(1)} %pad_clamp_fusion.1), kind=kCustom, calls=%fused_computation.3 | custom fusion | bytes 25165952 | tf_op jit(solution)/shard_map/gather | solution.py:35
  28.1 7.6 all-to-all-start
  39.6 5.9 broadcast_in_dim.35
  45.5 5.2 bitcast_dynamic-update-slice_fusion
  50.7 158.8 %all-to-all-done = bf16[32,256,768]{2,1,0:T(8,128)(2,1)} async-done(((bf16[32,256,768]{2,1,0:T(8,128)(2,1)}), bf16[32,256,768]{2,1,0:T(8,128)(2,1)}, u32[]{:S(2)}, u32[]{:S(2)}) %all-to-all-start) | async-done | bytes 12582944 | tf_op jit(solution)/shard_map/all_to_all | solution.py:36
  209.4 5.9 broadcast_in_dim.37
  215.3 158.0 %while.12 = (s32[]{:T(128)}, f32[16,256,768]{2,1,0:T(8,128)}, bf16[32,256,768]{2,1,0:T(8,128)(2,1)}, s32[]{:T(128)}, s32[32]{0:T(128)S(1)}, /*index=5*/s32[32,4]...) while((s32[]{:T(128)}, f32[16,256,768]{2,1,0:T(8,128)}, ...), condition=%wide.region_5.6_spmd, body=%wide.region_3.5_spmd.sunk | while | flops 1210516480 | bytes 30019964 | solution.py:72
  219.7 3.4 gather_fusion
  228.3 6.6 scatter_fusion
  242.2 3.4 gather_fusion
  250.7 6.6 scatter_fusion
  264.7 3.4 gather_fusion
  273.2 6.6 scatter_fusion
  287.1 3.4 gather_fusion
  295.7 6.6 scatter_fusion
  309.6 3.4 gather_fusion
  318.2 6.6 scatter_fusion
  324.7 3.0 fusion.60
  332.0 3.4 gather_fusion
  340.6 6.6 scatter_fusion
  347.2 3.0 fusion.60
  354.6 3.4 gather_fusion
  363.1 6.7 scatter_fusion
  369.8 3.0 fusion.60
  373.4 173.0 %all_to_all.10 = bf16[32,256,768]{2,1,0:T(8,128)(2,1)S(1)} all-to-all(bf16[32,256,768]{2,1,0:T(8,128)(2,1)} %get-tuple-element.57), channel_id=1, replica_groups=mesh['rows'=32,'grp'=4] {'rows'}, dimensions={0} | all-to-all | bytes 25165824 | tf_op jit(solution)/shard_map/all_to_all | solution.py:73
  546.3 9.0 %convert_element_type.28 = f32[32,256,768]{2,1,0:T(8,128)} convert(bf16[32,256,768]{2,1,0:T(8,128)(2,1)S(1)} %all_to_all.10) | non-fusion elementwise | flops 6291456 | bytes 37748736 | tf_op jit(solution)/shard_map/convert_element_type | solution.py:74
  555.4 56.5 %scatter_fusion.1 = f32[16,256,768]{2,1,0:T(8,128)} fusion(f32[16,256,768]{2,1,0:T(8,128)} %get-tuple-element.56, s32[32]{0:T(128)S(1)} %get-tuple-element.97, f32[32,256,768]{2,1,0:T(8,128)} %convert_element_type.28), kind=kCustom, calls=%fused_computation.5 | custom fusion | flops 6291456 | bytes 75497600 | tf_op jit(solution)/shard_map/scatter-add | solution.py:74
  611.9 227.6 %all-reduce.2.cloned.1.call-done = f32[16,256,768]{2,1,0:T(8,128)} async-done(((f32[16,256,768]{2,1,0:T(8,128)}), f32[16,256,768]{2,1,0:T(8,128)}) %all-reduce.2.cloned.1.call-update) | async-done | bytes 12582928 | tf_op jit(solution)/shard_map/psum | solution.py:75
  839.5 5.5 multiply_reduce_fusion
  845.0 8.0 multiply_convert_fusion
  (102 shorter events, 64.7 us)
Async XLA Ops:
  28.1 7.7 copy-start.3
  28.1 7.8 copy-start
  28.1 181.4 %all-to-all-start = ((bf16[32,256,768]{2,1,0:T(8,128)(2,1)}), bf16[32,256,768]{2,1,0:T(8,128)(2,1)}, u32[]{:S(2)}, u32[]{:S(2)}) async-start(bf16[32,256,768]{2,1,0:T(8,128)(2,1)} %gather_fusion.3), calls=%async_computation | async-start | bytes 25165824 | tf_op jit(solution)/shard_map/all_to_all | solution.py:36
  35.7 803.8 %all-reduce.2.cloned.1.call-start = ((), (), s32[]{:S(2)}) async-start(), calls=%async_computation.2 | async-start | bytes 25165824 | tf_op jit(solution)/shard_map/psum | solution.py:75
  223.2 1.1 copy-start.1
  225.9 0.8 copy-start.2
  245.6 1.1 copy-start.1
  248.4 0.8 copy-start.2
  268.1 1.1 copy-start.1
  270.9 0.8 copy-start.2
  290.6 1.1 copy-start.1
  293.3 0.8 copy-start.2
  313.1 1.1 copy-start.1
  315.8 0.8 copy-start.2
  335.5 1.1 copy-start.1
  338.2 0.8 copy-start.2
  358.0 1.1 copy-start.1
  360.8 0.8 copy-start.2
Sparse Core Ops, SparseCore 0:
  612.0 227.4 all-reduce.1
where the time goes:
time: 864 us; the launch traced here: 860 us
  waiting for transfers between devices  386 us (45%)
  blocking collectives  173 us (20%)
  other arithmetic  144 us (17%)
  local copies, waits for them, and re-layouts  68.5 us (8%)
  matrix products  48 us (6%)
  loops' own time  18.6 us (2%)
  between operations  13.5 us (2%)
    psum x1, waiting for transfers between devices, on_device(): summed = lax.psum(totals, 'grp')  228 us
    all_to_all x1, blocking collectives, on_device(): lax.all_to_all(returned, 'rows', split_axis=0, concat_axis=0, tiled=True)  173 us
    all_to_all x1, waiting for transfers between devices, on_device(): lax.all_to_all(outgoing, 'rows', split_axis=0, concat_axis=0, tiled=True)  159 us
    scatter-add x1, other arithmetic, on_device(): totals = totals.at[wanted].add(came_back.astype(jnp.float32))  56.5 us
    scatter-add x7, other arithmetic, visit(): totals_now = totals_now.at[picked].add(forward)  46.3 us
    gather x7, local copies, waits for them, and re-layouts, visit(): own_blocks = blocks[picked]  24 us
    dot_general x7, matrix products, visit(): jnp.einsum('kab,kad->bd', pair_weight, own_blocks, preferred_element_type...  20.6 us
    another operation x1, loops' own time, on_device(): totals, returned = lax.fori_loop(0, visit_count, visit, (totals, returned))  18.6 us
  transfers between devices with their start and end apart: 2, of which 2 were waited for; matrix products, arithmetic and copies ran while one was open for 2% of the time, Pallas kernels for 0%

commit v1 on v0

v1 whole, which is shorter than its diff:
```python
import functools

import jax
import jax.numpy as jnp
from jax import lax
from jax.experimental import pallas as pl
from jax.experimental.pallas import tpu as pltpu
from jax.sharding import PartitionSpec as P

BLOCK = 256
FEATURES = 768
BLK_DEV = 16
LINKS = 4
GROUPS = 4
SLOTS = 8
CHUNKS = 4
CHUNK_ROWS = BLOCK // CHUNKS
PIECE = 16
MESH = pl.DeviceIdType.MESH


def peer_at(me, group, slot, sign):
    step_x = slot // 2
    step_y = step_x + group
    flip = slot % 2
    x, y, core = me // 8, (me // 2) % 4, me % 2
    return ((x + sign * step_x + 8) % 4) * 8 + ((y + sign * step_y + 8) % 4) * 2 + (core + flip) % 2


def is_remote(group, slot):
    return jnp.logical_or(group != 0, slot != 0)


def row_scaled(values):
    return values * lax.rsqrt(jnp.mean(values * values, axis=-1, keepdims=True) + 1e-06)


def fetch_kernel(wanted, emb, normed, fetched, raw, nb, out, in_sem, norm_sem, send_sem, recv_sem):
    me = lax.axis_index("rows")
    group = lax.axis_index("grp")

    for b in range(BLK_DEV):
        pltpu.make_async_copy(emb.at[b], raw.at[b], in_sem.at[b]).start()

    barrier = pltpu.get_barrier_semaphore()

    def greet(slot, carry):
        @pl.when(is_remote(group, slot))
        def _():
            pl.semaphore_signal(
                barrier, inc=1, device_id={"rows": peer_at(me, group, slot, -1)}, device_id_type=MESH
            )

        return carry

    lax.fori_loop(0, SLOTS, greet, 0)

    def normalise(b, carry):
        pltpu.make_async_copy(emb.at[b], raw.at[b], in_sem.at[b]).wait()
        nb[b] = row_scaled(raw[b].astype(jnp.float32)).astype(jnp.bfloat16)
        pltpu.make_async_copy(nb.at[b], normed.at[b], norm_sem.at[b]).start()
        return carry

    lax.fori_loop(0, BLK_DEV, normalise, 0)
    pl.semaphore_wait(barrier, jnp.where(group == 0, SLOTS - 1, SLOTS))

    def remote(slot):
        return pltpu.make_async_remote_copy(
            src_ref=out.at[slot],
            dst_ref=fetched.at[slot],
            send_sem=send_sem.at[slot],
            recv_sem=recv_sem.at[slot],
            device_id={"rows": peer_at(me, group, slot, 1)},
            device_id_type=MESH,
        )

    def send(slot, carry):
        @pl.when(is_remote(group, slot))
        def _():
            out[slot] = nb[wanted[peer_at(me, group, slot, 1)]]
            remote(slot).start()

        return carry

    lax.fori_loop(0, SLOTS, send, 0)

    def finish(slot, carry):
        @pl.when(is_remote(group, slot))
        def _():
            remote(slot).wait()

        return carry

    lax.fori_loop(0, SLOTS, finish, 0)

    def written(b, carry):
        pltpu.make_async_copy(nb.at[b], normed.at[b], norm_sem.at[b]).wait()
        return carry

    lax.fori_loop(0, BLK_DEV, written, 0)


def cubed(cosines):
    weight = jnp.maximum(cosines * (1.0 / FEATURES), 0.0)
    return (weight * weight * weight).astype(jnp.bfloat16)


def nt_dot(left, right):
    return lax.dot_general(left, right, (((1,), (1,)), ((), ())), preferred_element_type=jnp.float32)


def tn_dot(left, right):
    return lax.dot_general(left, right, (((0,), (0,)), ((), ())), preferred_element_type=jnp.float32)


def pair_kernel(links, counts, normed, fetched, totals_out, back_out, nb, got, cat, totals, back, in_sem, got_sem,
                out_sem, back_sem):
    me = lax.axis_index("rows")
    group = lax.axis_index("grp")

    def load_block(b):
        return pltpu.make_async_copy(normed.at[b], nb.at[b], in_sem.at[b])

    def load_slot(slot):
        return pltpu.make_async_copy(fetched.at[slot], got.at[slot], got_sem.at[slot])

    def store_block(b):
        return pltpu.make_async_copy(totals.at[b], totals_out.at[b], out_sem.at[b])

    def store_slot(slot):
        return pltpu.make_async_copy(back.at[slot], back_out.at[slot], back_sem.at[slot])

    def start_block(b, carry):
        load_block(lax.rem(b + group * (BLK_DEV // GROUPS), BLK_DEV)).start()
        return carry

    lax.fori_loop(0, BLK_DEV, start_block, 0)

    def start_slot(slot, carry):
        load_slot(slot).start()
        return carry

    lax.fori_loop(0, SLOTS, start_slot, 0)

    def diagonal(i, carry):
        b = group * (BLK_DEV // GROUPS) + i
        load_block(b).wait()
        block = nb[b]
        totals[b] = jnp.dot(cubed(nt_dot(block, block)), block, preferred_element_type=jnp.float32)
        return carry

    lax.fori_loop(0, BLK_DEV // GROUPS, diagonal, 0)

    def clear(i, carry):
        b = lax.rem(group * (BLK_DEV // GROUPS) + i, BLK_DEV)
        load_block(b).wait()
        totals[b] = jnp.zeros((BLOCK, FEATURES), jnp.float32)
        return carry

    lax.fori_loop(BLK_DEV // GROUPS, BLK_DEV, clear, 0)

    def visit(slot, carry):
        peer = peer_at(me, group, slot, -1)
        count = jnp.where(is_remote(group, slot), counts[peer], 0)
        load_slot(slot).wait()

        @pl.when(count == 0)
        def _():
            back[slot] = jnp.zeros((BLOCK, FEATURES), jnp.bfloat16)

        def linked(n):
            for j in range(n):
                cat[pl.ds(j * BLOCK, BLOCK)] = nb[links[peer * LINKS + j]]
            own = cat[pl.ds(0, n * BLOCK)]
            remote = got[slot]
            weight = cubed(nt_dot(own, remote))
            back[slot] = tn_dot(weight, own).astype(jnp.bfloat16)
            for j in range(n):
                picked = links[peer * LINKS + j]
                totals[picked] += jnp.dot(
                    weight[j * BLOCK:(j + 1) * BLOCK], remote, preferred_element_type=jnp.float32
                )

        for n in range(1, LINKS + 1):
            pl.when(count == n)(functools.partial(linked, n))
        store_slot(slot).start()
        return carry

    lax.fori_loop(0, SLOTS, visit, 0)

    def start_store(b, carry):
        store_block(b).start()
        return carry

    lax.fori_loop(0, BLK_DEV, start_store, 0)

    def end_store(b, carry):
        store_block(b).wait()
        return carry

    lax.fori_loop(0, BLK_DEV, end_store, 0)

    def end_slot(slot, carry):
        store_slot(slot).wait()
        return carry

    lax.fori_loop(0, SLOTS, end_slot, 0)


def combine_kernel(wanted, part, back, refined, spread, returned, part_buf, total, own, step_in, step_out, owner_in,
                   final, part_sem, back_send, back_recv, step_send, step_recv, direct_send, direct_recv, sum_send,
                   sum_recv, gather_send, gather_recv, pass_send, pass_recv, local_sem):
    me = lax.axis_index("rows")
    group = lax.axis_index("grp")
    right, left, across = (group + 1) % GROUPS, (group + 3) % GROUPS, (group + 2) % GROUPS
    per = BLK_DEV // GROUPS
    half = per // 2
    ends = (right, left)
    sides = (left, right)

    barrier = pltpu.get_barrier_semaphore()

    def greet(slot, carry):
        @pl.when(is_remote(group, slot))
        def _():
            pl.semaphore_signal(
                barrier, inc=1, device_id={"rows": peer_at(me, group, slot, 1)}, device_id_type=MESH
            )

        return carry

    lax.fori_loop(0, SLOTS, greet, 0)
    for end in ends:
        pl.semaphore_signal(barrier, inc=1, device_id={"grp": end}, device_id_type=MESH)

    def rows_of(t):
        return pl.ds(pl.multiple_of(t * CHUNK_ROWS, CHUNK_ROWS), CHUNK_ROWS)

    def part_copy(t):
        return pltpu.make_async_copy(part.at[:, rows_of(t)], part_buf.at[t % 2], part_sem.at[t % 2])

    part_copy(0).start()

    row_id = lax.broadcasted_iota(jnp.int32, (BLK_DEV * PIECE, SLOTS * PIECE), 0)
    col_id = lax.broadcasted_iota(jnp.int32, (BLK_DEV * PIECE, SLOTS * PIECE), 1)
    hot = jnp.zeros((BLK_DEV * PIECE, SLOTS * PIECE), jnp.float32)
    for slot in range(SLOTS):
        block_id = wanted[peer_at(me, group, slot, 1)]
        hit = jnp.where(row_id == block_id * PIECE + (col_id - slot * PIECE), 1.0, 0.0)
        inside = jnp.where(col_id >= slot * PIECE, 1.0, 0.0) * jnp.where(col_id < (slot + 1) * PIECE, 1.0, 0.0)
        hot = hot + hit * inside
    spread[...] = hot.astype(jnp.bfloat16)

    @pl.when(group == 0)
    def _():
        for t in range(CHUNKS):
            returned[t, 0] = jnp.zeros((CHUNK_ROWS, FEATURES), jnp.bfloat16)

    pl.semaphore_wait(barrier, jnp.where(group == 0, SLOTS - 1, SLOTS) + 2)

    def back_copy(t, slot):
        return pltpu.make_async_remote_copy(
            src_ref=back.at[slot, rows_of(t)],
            dst_ref=returned.at[t, slot],
            send_sem=back_send.at[t, slot],
            recv_sem=back_recv.at[t, slot],
            device_id={"rows": peer_at(me, group, slot, -1)},
            device_id_type=MESH,
        )

    def each_back(action):
        def one(i, carry):
            t, slot = i // SLOTS, i % SLOTS

            @pl.when(is_remote(group, slot))
            def _():
                action(back_copy(t, slot))

            return carry

        return one

    lax.fori_loop(0, CHUNKS * SLOTS, each_back(lambda copy: copy.start()), 0)

    def along(src, dst, send, recv, t, way):
        return pltpu.make_async_remote_copy(
            src_ref=src, dst_ref=dst, send_sem=send.at[t, way], recv_sem=recv.at[t, way],
            device_id={"grp": ends[way]}, device_id_type=MESH,
        )

    def step_copy(t, way):
        return along(total.at[t, pl.ds(across * per + way * half, half)], step_in.at[t, way], step_send, step_recv,
                     t, way)

    def direct_copy(t, way):
        spot = (1 - way) * half
        return along(total.at[t, pl.ds(ends[way] * per + spot, half)], owner_in.at[t, way, pl.ds(spot, half)],
                     direct_send, direct_recv, t, way)

    def sum_copy(t, way):
        return along(step_out.at[t, way], owner_in.at[t, way, pl.ds(way * half, half)], sum_send, sum_recv, t, way)

    def gather_copy(t, way):
        return along(final.at[t], refined.at[pl.ds(group * per, per), rows_of(t)], gather_send, gather_recv, t, way)

    def pass_copy(t, way):
        spot = refined.at[pl.ds(sides[way] * per + way * half, half), rows_of(t)]
        return along(spot, spot, pass_send, pass_recv, t, way)

    def local_copy(t):
        return pltpu.make_async_copy(final.at[t], refined.at[pl.ds(group * per, per), rows_of(t)], local_sem.at[t])

    def tick(t, carry):
        @pl.when(t < CHUNKS)
        def _():
            now = t

            @pl.when(now + 1 < CHUNKS)
            def _():
                part_copy(now + 1).start()

            def arrived(slot, carry):
                @pl.when(is_remote(group, slot))
                def _():
                    back_copy(now, slot).wait_recv()

                return carry

            lax.fori_loop(0, SLOTS, arrived, 0)
            part_copy(now).wait()

            def piece(g, carry):
                rows = pl.ds(pl.multiple_of(g * PIECE, PIECE), PIECE)
                came = returned[now, :, rows, :].reshape(SLOTS * PIECE, FEATURES)
                sums = jnp.dot(spread[...], came, preferred_element_type=jnp.float32)
                sums = sums.reshape(BLK_DEV, PIECE, FEATURES) + part_buf[now % 2, :, rows, :]
                total[now, :, rows, :] = sums.astype(jnp.bfloat16)
                mine = jnp.dot(
                    spread[pl.ds(pl.multiple_of(group * per * PIECE, per * PIECE), per * PIECE), :], came,
                    preferred_element_type=jnp.float32,
                )
                own[now, :, rows, :] = (
                    mine.reshape(per, PIECE, FEATURES) + part_buf[now % 2, pl.ds(group * per, per), rows, :]
                )
                return carry

            lax.fori_loop(0, CHUNK_ROWS // PIECE, piece, 0)
            for way in range(2):
                step_copy(now, way).start()
            for way in range(2):
                direct_copy(now, way).start()

        @pl.when(jnp.logical_and(t >= 1, t < CHUNKS + 1))
        def _():
            now = t - 1
            for way in range(2):
                step_copy(now, way).wait_recv()
                mine = total[now, pl.ds(ends[way] * per + way * half, half)]
                step_out[now, way] = (
                    step_in[now, way].astype(jnp.float32) + mine.astype(jnp.float32)
                ).astype(jnp.bfloat16)
                sum_copy(now, way).start()

        @pl.when(jnp.logical_and(t >= 2, t < CHUNKS + 2))
        def _():
            now = t - 2
            for way in range(2):
                direct_copy(now, way).wait_recv()
                sum_copy(now, way).wait_recv()
            for k in range(per):
                summed = (
                    own[now, k] + owner_in[now, 0, k].astype(jnp.float32) + owner_in[now, 1, k].astype(jnp.float32)
                )
                final[now, k] = row_scaled(summed).astype(jnp.bfloat16)
            for way in range(2):
                gather_copy(now, way).start()
            local_copy(now).start()

        @pl.when(t >= 3)
        def _():
            now = t - 3
            for way in range(2):
                gather_copy(now, way).wait_recv()
                pass_copy(now, way).start()

        return carry

    lax.fori_loop(0, CHUNKS + 3, tick, 0)

    def finish(t, carry):
        for way in range(2):
            pass_copy(t, way).wait_recv()
            step_copy(t, way).wait_send()
            direct_copy(t, way).wait_send()
            sum_copy(t, way).wait_send()
            gather_copy(t, way).wait_send()
            pass_copy(t, way).wait_send()
        local_copy(t).wait()
        return carry

    lax.fori_loop(0, CHUNKS, finish, 0)
    lax.fori_loop(0, CHUNKS * SLOTS, each_back(lambda copy: copy.wait_send()), 0)


def on_device(embeddings, partner, links, counts):
    blocks = (BLK_DEV, BLOCK, FEATURES)
    slots = (SLOTS, BLOCK, FEATURES)
    wanted = partner.reshape(-1)
    my_links = links.reshape(-1)
    my_counts = counts.reshape(-1)
    smem = pl.BlockSpec(memory_space=pltpu.SMEM)
    anywhere = pl.BlockSpec(memory_space=pl.ANY)
    dma = pltpu.SemaphoreType.DMA
    normed, fetched = pl.pallas_call(
        fetch_kernel,
        out_shape=(jax.ShapeDtypeStruct(blocks, jnp.bfloat16), jax.ShapeDtypeStruct(slots, jnp.bfloat16)),
        in_specs=[smem, anywhere],
        out_specs=(anywhere, anywhere),
        scratch_shapes=[
            pltpu.VMEM(blocks, jnp.bfloat16),
            pltpu.VMEM(blocks, jnp.bfloat16),
            pltpu.VMEM(slots, jnp.bfloat16),
            dma((BLK_DEV,)),
            dma((BLK_DEV,)),
            dma((SLOTS,)),
            dma((SLOTS,)),
        ],
        compiler_params=pltpu.CompilerParams(
            collective_id=0, has_side_effects=True, vmem_limit_bytes=40 * 2**20
        ),
        name="fetch",
    )(wanted, embeddings.reshape(blocks))
    part, back = pl.pallas_call(
        pair_kernel,
        out_shape=(jax.ShapeDtypeStruct(blocks, jnp.float32), jax.ShapeDtypeStruct(slots, jnp.bfloat16)),
        in_specs=[smem, smem, anywhere, anywhere],
        out_specs=(anywhere, anywhere),
        scratch_shapes=[
            pltpu.VMEM(blocks, jnp.bfloat16),
            pltpu.VMEM(slots, jnp.bfloat16),
            pltpu.VMEM((LINKS * BLOCK, FEATURES), jnp.bfloat16),
            pltpu.VMEM(blocks, jnp.float32),
            pltpu.VMEM(slots, jnp.bfloat16),
            dma((BLK_DEV,)),
            dma((SLOTS,)),
            dma((BLK_DEV,)),
            dma((SLOTS,)),
        ],
        compiler_params=pltpu.CompilerParams(vmem_limit_bytes=50 * 2**20),
        name="pairs",
    )(my_links, my_counts, normed, fetched)
    per = BLK_DEV // GROUPS
    refined = pl.pallas_call(
        combine_kernel,
        out_shape=jax.ShapeDtypeStruct(blocks, jnp.bfloat16),
        in_specs=[smem, anywhere, anywhere],
        out_specs=anywhere,
        scratch_shapes=[
            pltpu.VMEM((BLK_DEV * PIECE, SLOTS * PIECE), jnp.bfloat16),
            pltpu.VMEM((CHUNKS, SLOTS, CHUNK_ROWS, FEATURES), jnp.bfloat16),
            pltpu.VMEM((2, BLK_DEV, CHUNK_ROWS, FEATURES), jnp.float32),
            pltpu.VMEM((CHUNKS, BLK_DEV, CHUNK_ROWS, FEATURES), jnp.bfloat16),
            pltpu.VMEM((CHUNKS, per, CHUNK_ROWS, FEATURES), jnp.float32),
            pltpu.VMEM((CHUNKS, 2, per // 2, CHUNK_ROWS, FEATURES), jnp.bfloat16),
            pltpu.VMEM((CHUNKS, 2, per // 2, CHUNK_ROWS, FEATURES), jnp.bfloat16),
            pltpu.VMEM((CHUNKS, 2, per, CHUNK_ROWS, FEATURES), jnp.bfloat16),
            pltpu.VMEM((CHUNKS, per, CHUNK_ROWS, FEATURES), jnp.bfloat16),
            dma((2,)),
            dma((CHUNKS, SLOTS)),
            dma((CHUNKS, SLOTS)),
        ] + [dma((CHUNKS, 2))] * 10 + [dma((CHUNKS,))],
        compiler_params=pltpu.CompilerParams(
            collective_id=1, has_side_effects=True, vmem_limit_bytes=50 * 2**20
        ),
        name="combine",
    )(wanted, part, back)
    return refined.reshape(BLK_DEV * BLOCK, FEATURES)


def solution(mesh):
    placed = (P("rows", None), P(None, "rows"), P("rows", None, None), P("rows", None))
    return jax.shard_map(
        on_device, mesh=mesh, in_specs=placed, out_specs=P("rows", None), check_vma=False
    )
```

time: 864 us -> 235 us (0.27)
  waiting for transfers between devices: 386 us -> 0 us
  Pallas kernels: 0 us -> 223 us
  blocking collectives: 173 us -> 0 us
  other arithmetic: 144 us -> 0 us
  local copies, waits for them, and re-layouts: 68.5 us -> 11.8 us
  matrix products: 48 us -> 0 us
  loops' own time: 18.6 us -> 0 us
  between operations: 13.5 us -> 0.06 us
    psum x1 -> x0, waiting for transfers between devices: 228 us -> none  [on_device(): summed = lax.psum(totals, 'grp')]
    pallas_call x0 -> x3, Pallas kernels: none -> 223 us  [the longest x1 142 us: on_device(): pl.pallas_call(combine_kernel, out_shape=jax.ShapeDtypeStruct(blocks, jnp...]
    all_to_all x1 -> x0, blocking collectives: 173 us -> none  [on_device(): lax.all_to_all(returned, 'rows', split_axis=0, concat_axis=0, tiled=True)]
    all_to_all x1 -> x0, waiting for transfers between devices: 159 us -> none  [on_device(): lax.all_to_all(outgoing, 'rows', split_axis=0, concat_axis=0, tiled=True)]
    scatter-add x8 -> x0, other arithmetic: 103 us -> none  [the longest x1 56.5 us: on_device(): totals = totals.at[wanted].add(came_back.astype(jnp.float32))]
    dot_general x22 -> x0, matrix products: 48 us -> none  [the longest x7 20.6 us: visit(): jnp.einsum('kab,kad->bd', pair_weight, own_blocks, preferred_element_type...]
    gather x10 -> x0, local copies, waits for them, and re-layouts: 34.9 us -> none  [the longest x7 24 us: visit(): own_blocks = blocks[picked]]
    convert_element_type x3 -> x0, other arithmetic: 24.3 us -> none  [the longest x1 9.02 us: on_device(): totals = totals.at[wanted].add(came_back.astype(jnp.float32))]
  transfers between devices with their start and end apart: 2 -> 0, of which waited for: 2 -> 0; matrix products, arithmetic and copies ran while one was open for 2% -> 0% of each run, Pallas kernels for 0% -> 0%
where the time goes in v1:
time: 235 us
  Pallas kernels  223 us (95%)
  local copies, waits for them, and re-layouts  11.8 us (5%)
    pallas_call x1, Pallas kernels, on_device(): pl.pallas_call(combine_kernel, out_shape=jax.ShapeDtypeStruct(blocks, jnp...  142 us
    pallas_call x1, Pallas kernels, on_device(): pl.pallas_call(fetch_kernel, out_shape=(jax.ShapeDtypeStruct(blocks, jnp....  62.1 us
    pallas_call x1, Pallas kernels, on_device(): pl.pallas_call(pair_kernel, out_shape=(jax.ShapeDtypeStruct(blocks, jnp.f...  19.3 us
    unnamed x12, local copies, waits for them, and re-layouts  11.7 us

profile of v1, /device:TPU:14, one launch (start us, length us, event | category | flops | bytes accessed | tf_op | source)
XLA Modules:
  0.0 235.0 jit_solution(10339394000864387587)
XLA Ops:
  0.0 0.0 copy-start.4
  0.0 0.8 copy.6
  0.8 0.1 reshape.16.links
  0.9 0.0 copy-start.2
  0.9 0.6 copy-done.2
  1.5 62.1 %fetch.1 = (bf16[16,256,768]{2,1,0:T(8,128)(2,1)S(1)}, bf16[8,256,768]{2,1,0:T(8,128)(2,1)S(1)}) custom-call(s32[32]{0:T(128)S(1)} %bitcast.4, bf16[16,256,768]{2,1,0:T(8,128)(2,1)} %bitcast.8), custom_call_target="tpu_custom_call" | custom-call | tf_op jit(solution)/shard_map/fetch/pallas_call | solution.py:414
  63.6 0.0 copy-start
  63.6 2.7 %copy-done = bf16[16,256,768]{2,1,0:T(8,128)(2,1)} copy-done((bf16[16,256,768]{2,1,0:T(8,128)(2,1)}, bf16[16,256,768]{2,1,0:T(8,128)(2,1)S(1)}, u32[]{:S(2)}) %copy-start) | copy-done | bytes 6291480
  66.3 0.0 copy-start.1
  66.3 1.6 copy-done.1
  68.0 0.0 copy-start.3
  68.0 0.0 copy-done.4
  68.0 19.3 %pairs.1 = (f32[16,256,768]{2,1,0:T(8,128)}, bf16[8,256,768]{2,1,0:T(8,128)(2,1)S(1)}) custom-call(s32[128]{0:T(128)S(1)} %reshape.16.links, s32[32]{0:T(128)S(1)} %bitcast.6, bf16[16,256,768]{2,1,0:T(8,128)(2,1)} %copy-done, bf16[8,256,768]{2,1,0:T(8,128)(2,1)} %copy-done.1), custom_call_target="tpu_custom_call" | custom-call | tf_op jit(solution)/shard_map/pairs/pallas_call | solution.py:433
  87.3 0.0 copy-done.3
  87.3 141.8 %combine.1 = bf16[16,256,768]{2,1,0:T(8,128)(2,1)} custom-call(s32[32]{0:T(128)S(1)} %bitcast.5, f32[16,256,768]{2,1,0:T(8,128)} %get-tuple-element.11.part, bf16[8,256,768]{2,1,0:T(8,128)(2,1)S(1)} %get-tuple-element.12.back), custom_call_target="tpu_custom_call" | custom-call | tf_op jit(solution)/shard_map/combine/pallas_call | solution.py:453
  229.1 5.9 %copy.8 = bf16[4096,768]{1,0:T(8,128)(2,1)} copy(bf16[4096,768]{1,0:T(8,128)(2,1)} %bitcast.7) | data formatting | bytes 12582912
Async XLA Ops:
  0.0 68.0 %copy-start.4 = (s32[1,32]{1,0:T(1,128)S(1)}, s32[1,32]{1,0:T(1,128)}, u32[]{:S(2)}) copy-start(s32[1,32]{1,0:T(1,128)} %param.7) | copy-start | bytes 388
  0.9 0.7 copy-start.2
  63.6 2.7 %copy-start = (bf16[16,256,768]{2,1,0:T(8,128)(2,1)}, bf16[16,256,768]{2,1,0:T(8,128)(2,1)S(1)}, u32[]{:S(2)}) copy-start(bf16[16,256,768]{2,1,0:T(8,128)(2,1)S(1)} %get-tuple-element.9.normed) | copy-start | bytes 18874372
  66.3 1.6 copy-start.1
  68.0 19.3 %copy-start.3 = (s32[32,1]{0,1:T(1,128)S(1)}, s32[32,1]{0,1:T(1,128)}, u32[]{:S(2)}) copy-start(s32[32,1]{0,1:T(1,128)} %param.5) | copy-start | bytes 388

commit v2 on v0

v2 whole, which is shorter than its diff:
```python
import jax
import jax.numpy as jnp
from jax import lax
from jax.experimental import pallas as pl
from jax.experimental.pallas import tpu as pltpu
from jax.sharding import PartitionSpec as P

BLOCK = 256
FEATURES = 768
BLK_DEV = 16
LINKS = 4
GROUPS = 4
SLOTS = 8
SELF_SLOT = 6
TERMS = SLOTS * LINKS + SLOTS
CHUNKS = 4
CHUNK_ROWS = BLOCK // CHUNKS
PIECE = 16
MESH = pl.DeviceIdType.MESH


def slot_step(group, slot):
    turn = slot // 2
    ties_first = jnp.where(turn == 0, 2, jnp.where(turn == 1, 1, jnp.where(turn == 2, 3, 0)))
    step_x = jnp.where(group <= 1, ties_first, jnp.where(group == 2, turn, (turn + 2) % 4))
    return step_x, (step_x + group) % 4, slot % 2


def peer_at(me, group, slot, sign):
    step_x, step_y, flip = slot_step(group, slot)
    x, y, core = me // 8, (me // 2) % 4, me % 2
    return ((x + sign * step_x + 4) % 4) * 8 + ((y + sign * step_y + 4) % 4) * 2 + (core + flip) % 2


def is_remote(group, slot):
    return jnp.logical_or(group != 0, slot != SELF_SLOT)


def row_scaled(values):
    return values * lax.rsqrt(jnp.mean(values * values, axis=-1, keepdims=True) + 1e-06)


def cubed_float(cosines):
    weight = jnp.maximum(cosines * (1.0 / FEATURES), 0.0)
    return weight * weight * weight


def cubed(cosines):
    return cubed_float(cosines).astype(jnp.bfloat16)


def nt_dot(left, right):
    return lax.dot_general(left, right, (((1,), (1,)), ((), ())), preferred_element_type=jnp.float32)


def tn_dot(left, right):
    return lax.dot_general(left, right, (((0,), (0,)), ((), ())), preferred_element_type=jnp.float32)


def whole_kernel(wanted, links, counts, emb, refined, nb, out, fetched, cat, forward, back, spread, returned, terms, total,
                 own, step_in, step_out, owner_in, final, in_sem, fetch_send, fetch_recv, back_send, back_recv,
                 step_send, step_recv, direct_send, direct_recv, sum_send, sum_recv, gather_send, gather_recv,
                 pass_send, pass_recv, local_sem):
    me = lax.axis_index("rows")
    group = lax.axis_index("grp")
    right, left, across = (group + 1) % GROUPS, (group + 3) % GROUPS, (group + 2) % GROUPS
    per = BLK_DEV // GROUPS
    half = per // 2
    ends = (right, left)
    sides = (left, right)
    partners = jnp.where(group == 0, SLOTS - 1, SLOTS)

    def each(count, action):
        def one(i, carry):
            action(i)
            return carry

        lax.fori_loop(0, count, one, 0)

    def each_remote(action):
        def one(slot):
            @pl.when(is_remote(group, slot))
            def _():
                action(slot)

        each(SLOTS, one)

    def emb_copy(b):
        return pltpu.make_async_copy(emb.at[b], nb.at[b], in_sem.at[b])

    each(BLK_DEV, lambda b: emb_copy(b).start())
    barrier = pltpu.get_barrier_semaphore()

    def greet(slot):
        for sign in (1, -1):
            pl.semaphore_signal(
                barrier, inc=1, device_id={"rows": peer_at(me, group, slot, sign)}, device_id_type=MESH
            )

    each_remote(greet)
    for end in ends:
        pl.semaphore_signal(barrier, inc=1, device_id={"grp": end}, device_id_type=MESH)

    def normalise(b):
        emb_copy(b).wait()
        nb[b] = row_scaled(nb[b].astype(jnp.float32)).astype(jnp.bfloat16)

    each(BLK_DEV, normalise)

    @pl.when(group == 0)
    def _():
        fetched[SELF_SLOT] = jnp.zeros((BLOCK, FEATURES), jnp.bfloat16)
        for t in range(CHUNKS):
            returned[t, SELF_SLOT] = jnp.zeros((CHUNK_ROWS, FEATURES), jnp.bfloat16)

    pl.semaphore_wait(barrier, 2 * partners + 2)

    def fetch_copy(slot):
        return pltpu.make_async_remote_copy(
            src_ref=out.at[slot],
            dst_ref=fetched.at[slot],
            send_sem=fetch_send.at[slot],
            recv_sem=fetch_recv.at[slot],
            device_id={"rows": peer_at(me, group, slot, 1)},
            device_id_type=MESH,
        )

    def send(slot):
        out[slot] = nb[wanted[peer_at(me, group, slot, 1)]]
        fetch_copy(slot).start()

    each_remote(send)

    def diagonal(k):
        block = nb[group * per + k]
        own[k] = jnp.dot(cubed(nt_dot(block, block)), block, preferred_element_type=jnp.float32)

    each(per, diagonal)

    col = lax.broadcasted_iota(jnp.int32, (8, TERMS * PIECE), 1)
    takes = jnp.zeros((8, TERMS * PIECE), jnp.int32)
    for slot in range(SLOTS):
        lister = peer_at(me, group, slot, 1)
        listed = peer_at(me, group, slot, -1)
        for j in range(LINKS):
            takes = jnp.where(col // PIECE == slot * LINKS + j, links[listed * LINKS + j], takes)
        takes = jnp.where(col // PIECE == SLOTS * LINKS + slot, wanted[lister], takes)
    row_id = lax.broadcasted_iota(jnp.int32, (BLK_DEV * PIECE, TERMS * PIECE), 0)
    col_id = lax.broadcasted_iota(jnp.int32, (BLK_DEV * PIECE, TERMS * PIECE), 1)
    spread[...] = jnp.where(row_id == takes[0:1] * PIECE + col_id % PIECE, 1.0, 0.0).astype(jnp.bfloat16)

    def rows_of(t):
        return pl.ds(pl.multiple_of(t * CHUNK_ROWS, CHUNK_ROWS), CHUNK_ROWS)

    def back_copy(t, slot):
        return pltpu.make_async_remote_copy(
            src_ref=back.at[slot, rows_of(t)],
            dst_ref=returned.at[t, slot],
            send_sem=back_send.at[t, slot],
            recv_sem=back_recv.at[t, slot],
            device_id={"rows": peer_at(me, group, slot, -1)},
            device_id_type=MESH,
        )

    row_number = lax.broadcasted_iota(jnp.int32, (LINKS * BLOCK, BLOCK), 0)

    def visit(slot):
        peer = peer_at(me, group, slot, -1)

        @pl.when(is_remote(group, slot))
        def _():
            fetch_copy(slot).wait_recv()

        for j in range(LINKS):
            cat[j * BLOCK:(j + 1) * BLOCK] = nb[links[peer * LINKS + j]]
        remote = fetched[slot]
        weight = jnp.where(
            row_number < counts[peer] * BLOCK, cubed_float(nt_dot(cat[...], remote)), 0.0
        ).astype(jnp.bfloat16)
        back[slot] = tn_dot(weight, cat[...]).astype(jnp.bfloat16)

        @pl.when(is_remote(group, slot))
        def _():
            back_copy(0, slot).start()

        for j in range(LINKS):
            forward[slot * LINKS + j] = jnp.dot(
                weight[j * BLOCK:(j + 1) * BLOCK], remote, preferred_element_type=jnp.float32
            ).astype(jnp.bfloat16)

    each(SLOTS, visit)
    for t in range(1, CHUNKS):
        each_remote(lambda slot: back_copy(t, slot).start())

    def along(src, dst, send, recv, t, way):
        return pltpu.make_async_remote_copy(
            src_ref=src, dst_ref=dst, send_sem=send.at[t, way], recv_sem=recv.at[t, way],
            device_id={"grp": ends[way]}, device_id_type=MESH,
        )

    def step_copy(t, way):
        return along(total.at[t, pl.ds(across * per + way * half, half)], step_in.at[t, way], step_send, step_recv,
                     t, way)

    def direct_copy(t, way):
        spot = (1 - way) * half
        return along(total.at[t, pl.ds(ends[way] * per + spot, half)], owner_in.at[t, way, pl.ds(spot, half)],
                     direct_send, direct_recv, t, way)

    def sum_copy(t, way):
        return along(step_out.at[t, way], owner_in.at[t, way, pl.ds(way * half, half)], sum_send, sum_recv, t, way)

    def gather_copy(t, way):
        return along(final.at[t], refined.at[pl.ds(group * per, per), rows_of(t)], gather_send, gather_recv, t, way)

    def pass_copy(t, way):
        spot = refined.at[pl.ds(sides[way] * per + way * half, half), rows_of(t)]
        return along(spot, spot, pass_send, pass_recv, t, way)

    def local_copy(t):
        return pltpu.make_async_copy(final.at[t], refined.at[pl.ds(group * per, per), rows_of(t)], local_sem.at[t])

    def tick(t, carry):
        @pl.when(t < CHUNKS)
        def _():
            now = t

            each_remote(lambda slot: back_copy(now, slot).wait_recv())

            def piece(g):
                rows = pl.ds(pl.multiple_of(g * PIECE, PIECE), PIECE)
                whole_rows = pl.ds(pl.multiple_of(now * CHUNK_ROWS + g * PIECE, PIECE), PIECE)
                terms[0:SLOTS * LINKS * PIECE] = forward[:, whole_rows, :].reshape(SLOTS * LINKS * PIECE, FEATURES)
                terms[SLOTS * LINKS * PIECE:] = returned[now, :, rows, :].reshape(SLOTS * PIECE, FEATURES)
                sums = jnp.dot(spread[...], terms[...], preferred_element_type=jnp.float32)
                total[now, :, rows, :] = sums.reshape(BLK_DEV, PIECE, FEATURES).astype(jnp.bfloat16)
                mine = jnp.dot(
                    spread[pl.ds(pl.multiple_of(group * per * PIECE, per * PIECE), per * PIECE), :], terms[...],
                    preferred_element_type=jnp.float32,
                )
                own[:, whole_rows, :] += mine.reshape(per, PIECE, FEATURES)

            each(CHUNK_ROWS // PIECE, piece)
            for way in range(2):
                step_copy(now, way).start()
            for way in range(2):
                direct_copy(now, way).start()

        @pl.when(jnp.logical_and(t >= 1, t < CHUNKS + 1))
        def _():
            now = t - 1
            for way in range(2):
                step_copy(now, way).wait_recv()
                mine = total[now, pl.ds(ends[way] * per + way * half, half)]
                step_out[now, way] = (
                    step_in[now, way].astype(jnp.float32) + mine.astype(jnp.float32)
                ).astype(jnp.bfloat16)
                sum_copy(now, way).start()

        @pl.when(jnp.logical_and(t >= 2, t < CHUNKS + 2))
        def _():
            now = t - 2
            for way in range(2):
                direct_copy(now, way).wait_recv()
                sum_copy(now, way).wait_recv()
            for k in range(per):
                summed = (
                    own[k, rows_of(now)] + owner_in[now, 0, k].astype(jnp.float32) + owner_in[now, 1, k].astype(jnp.float32)
                )
                final[now, k] = row_scaled(summed).astype(jnp.bfloat16)
            for way in range(2):
                gather_copy(now, way).start()
            local_copy(now).start()

        @pl.when(t >= 3)
        def _():
            now = t - 3
            for way in range(2):
                gather_copy(now, way).wait_recv()
                pass_copy(now, way).start()

        return carry

    lax.fori_loop(0, CHUNKS + 3, tick, 0)

    def finish(t, carry):
        for way in range(2):
            pass_copy(t, way).wait_recv()
            step_copy(t, way).wait_send()
            direct_copy(t, way).wait_send()
            sum_copy(t, way).wait_send()
            gather_copy(t, way).wait_send()
            pass_copy(t, way).wait_send()
        local_copy(t).wait()
        return carry

    lax.fori_loop(0, CHUNKS, finish, 0)
    each_remote(lambda slot: fetch_copy(slot).wait_send())
    for t in range(CHUNKS):
        each_remote(lambda slot: back_copy(t, slot).wait_send())


def on_device(embeddings, partner, links, counts):
    blocks = (BLK_DEV, BLOCK, FEATURES)
    slots = (SLOTS, BLOCK, FEATURES)
    per = BLK_DEV // GROUPS
    smem = pl.BlockSpec(memory_space=pltpu.SMEM)
    dma = pltpu.SemaphoreType.DMA

    def vmem(*shape):
        return pltpu.VMEM(shape + (FEATURES,), jnp.bfloat16)

    refined = pl.pallas_call(
        whole_kernel,
        out_shape=jax.ShapeDtypeStruct(blocks, jnp.bfloat16),
        in_specs=[smem, smem, smem, pl.BlockSpec(memory_space=pl.ANY)],
        out_specs=pl.BlockSpec(memory_space=pl.ANY),
        scratch_shapes=[
            vmem(BLK_DEV, BLOCK),
            vmem(SLOTS, BLOCK),
            vmem(SLOTS, BLOCK),
            vmem(LINKS * BLOCK),
            vmem(SLOTS * LINKS, BLOCK),
            vmem(SLOTS, BLOCK),
            pltpu.VMEM((BLK_DEV * PIECE, TERMS * PIECE), jnp.bfloat16),
            vmem(CHUNKS, SLOTS, CHUNK_ROWS),
            vmem(TERMS * PIECE),
            vmem(CHUNKS, BLK_DEV, CHUNK_ROWS),
            pltpu.VMEM((per, BLOCK, FEATURES), jnp.float32),
            vmem(CHUNKS, 2, per // 2, CHUNK_ROWS),
            vmem(CHUNKS, 2, per // 2, CHUNK_ROWS),
            vmem(CHUNKS, 2, per, CHUNK_ROWS),
            vmem(CHUNKS, per, CHUNK_ROWS),
            dma((BLK_DEV,)),
            dma((SLOTS,)),
            dma((SLOTS,)),
            dma((CHUNKS, SLOTS)),
            dma((CHUNKS, SLOTS)),
        ] + [dma((CHUNKS, 2))] * 10 + [dma((CHUNKS,))],
        compiler_params=pltpu.CompilerParams(
            collective_id=0, has_side_effects=True, vmem_limit_bytes=62 * 2**20
        ),
        name="whole",
    )(partner.reshape(-1), links.reshape(-1), counts.reshape(-1), embeddings.reshape(blocks))
    return refined.reshape(BLK_DEV * BLOCK, FEATURES)


def solution(mesh):
    placed = (P("rows", None), P(None, "rows"), P("rows", None, None), P("rows", None))
    return jax.shard_map(
        on_device, mesh=mesh, in_specs=placed, out_specs=P("rows", None), check_vma=False
    )
```

time: 864 us -> 185 us (0.21)
  the two profiles are of different devices: /device:TPU:14 before, /device:TPU:24 now
where the time goes in v2:
time: 185 us; the launch traced here: 184 us
  Pallas kernels  177 us (96%)
  local copies, waits for them, and re-layouts  7.27 us (4%)
    pallas_call x1, Pallas kernels, on_device(): pl.pallas_call(whole_kernel, out_shape=jax.ShapeDtypeStruct(blocks, jnp.b...  177 us
    unnamed x2, local copies, waits for them, and re-layouts  6.65 us

profile of v2, /device:TPU:24, one launch (start us, length us, event | category | flops | bytes accessed | tf_op | source)
XLA Modules:
  0.0 184.4 jit_solution(18290911431565875593)
XLA Ops:
  0.0 0.8 copy.6
  0.8 0.6 reshape.16.links
  1.4 177.1 %whole.1 = bf16[16,256,768]{2,1,0:T(8,128)(2,1)} custom-call(s32[32]{0:T(128)} %bitcast.6, s32[128]{0:T(128)} %reshape.16.links, s32[32]{0:T(128)} %bitcast.7, bf16[16,256,768]{2,1,0:T(8,128)(2,1)} %bitcast.5), custom_call_target="tpu_custom_call" | custom-call | tf_op jit(solution)/shard_map/whole/pallas_call | solution.py:313
  178.5 5.9 %copy.8 = bf16[4096,768]{1,0:T(8,128)(2,1)} copy(bf16[4096,768]{1,0:T(8,128)(2,1)} %bitcast.4) | data formatting | bytes 12582912

commit v3 on v0

v3 whole, which is shorter than its diff:
```python
import jax
import jax.numpy as jnp
from jax import lax
from jax.experimental import pallas as pl
from jax.experimental.pallas import tpu as pltpu
from jax.sharding import PartitionSpec as P

BLOCK = 256
FEATURES = 768
BLK_DEV = 16
HALF = BLK_DEV // 2
LINKS = 4
PLANES = 4
SLOTS = 16
ROUND = 4
CHUNKS = 4
CHUNK_ROWS = BLOCK // CHUNKS
PIECE = 16
NEAR = 6
MESH = pl.DeviceIdType.MESH


def slot_at(turn):
    diagonal, step = turn // 4, turn % 4
    ties_first = jnp.where(step == 0, 2, jnp.where(step == 1, 1, jnp.where(step == 2, 3, 0)))
    step_x = jnp.where(diagonal <= 1, ties_first, jnp.where(diagonal == 2, step, (step + 2) % 4))
    return step_x * 4 + (step_x + diagonal) % 4


def live_core(parity, plane):
    upper = (plane + 4 - parity) % 2
    return ((plane + 8 - upper - parity) % 4) // 2


def idle_side(slot, upper):
    step_x, step_y = slot // 4, slot % 4
    return jnp.where((step_x + step_y) % 2 == 0, (step_x + upper + 1) % 2, 0)


def crossed(slot, idle):
    step_x, step_y = slot // 4, slot % 4
    return jnp.where(idle == 1, (step_x + 1 - 2 * (step_x % 2)) * 4 + step_y + 1 - 2 * (step_y % 2), slot)


def row_scaled(values):
    return values * lax.rsqrt(jnp.mean(values * values, axis=-1, keepdims=True) + 1e-06)


def cubed(cosines):
    weight = jnp.maximum(cosines * (1.0 / FEATURES), 0.0)
    return weight * weight * weight


def nt_dot(left, right):
    return lax.dot_general(left, right, (((1,), (1,)), ((), ())), preferred_element_type=jnp.float32)


def tn_dot(left, right):
    return lax.dot_general(left, right, (((0,), (0,)), ((), ())), preferred_element_type=jnp.float32)


def whole_kernel(wanted, links, counts, emb, refined, nb, out, fetched, cat, forward, totals, back, spread, returned,
                 half_in, in_sem, fetch_send, fetch_recv, back_send, back_recv, half_send, half_recv, pair_send,
                 pair_recv, next_send, next_recv, near_send, near_recv, far_send, far_recv, local_sem):
    me = lax.axis_index("rows")
    plane = lax.axis_index("grp")
    x, y, core = me // 8, (me // 2) % 4, me % 2
    parity = (x + y) % 2
    role = (plane + 4 - (2 * core + parity)) % 4
    live = role < 2
    upper = (plane + 4 - parity) % 2
    mine = jnp.where(jnp.logical_or(role == 1, role == 2), 1, 0)
    inner = (plane + 5 - 2 * mine) % PLANES
    outer = (plane + 3 + 2 * mine) % PLANES

    def each(count, action):
        def one(i, carry):
            action(i)
            return carry

        lax.fori_loop(0, count, one, 0)

    def each_slot(action):
        def one(turn):
            slot = slot_at(turn)

            @pl.when(not_self(slot))
            def _():
                action(slot)

        each(SLOTS, one)

    def not_self(slot):
        return jnp.logical_or(slot != 0, upper == 0)

    def chip(slot, sign):
        step_x, step_y = slot // 4, slot % 4
        there = ((x + sign * step_x + 4) % 4) * 8 + ((y + sign * step_y + 4) % 4) * 2
        return there, (parity + step_x + step_y) % 2

    def owner_of(slot):
        there, kind = chip(slot, -1)
        return there + (live_core(kind, plane) + idle_side(slot, upper)) % 2

    def owner_plane(slot):
        return (plane + 4 + idle_side(slot, upper) * (2 * upper - 1)) % PLANES

    def taker_of(slot):
        there, kind = chip(slot, 1)
        return there + live_core(kind, plane)

    def lister_of(slot):
        there, kind = chip(crossed(slot, idle_side(slot, upper)), 1)
        return there + live_core(kind, owner_plane(slot))

    def emb_copy(b):
        return pltpu.make_async_copy(emb.at[b], nb.at[b], in_sem.at[b])

    each(BLK_DEV, lambda b: emb_copy(b).start())
    barrier = pltpu.get_barrier_semaphore()

    @pl.when(live)
    def _():
        def greet(slot):
            pl.semaphore_signal(
                barrier, inc=1, device_id={"rows": owner_of(slot), "grp": plane}, device_id_type=MESH
            )
            pl.semaphore_signal(
                barrier, inc=1, device_id={"rows": lister_of(slot), "grp": owner_plane(slot)}, device_id_type=MESH
            )

        each_slot(greet)

    for side in (inner, outer):
        pl.semaphore_signal(barrier, inc=1, device_id={"rows": me, "grp": side}, device_id_type=MESH)

    each(BLK_DEV, lambda b: emb_copy(b).wait())
    pl.semaphore_wait(barrier, jnp.where(live, 30 - 2 * upper, 6))

    def fetch_copy(slot):
        return pltpu.make_async_remote_copy(
            src_ref=out.at[slot],
            dst_ref=fetched.at[slot],
            send_sem=fetch_send.at[slot],
            recv_sem=fetch_recv.at[slot],
            device_id={"rows": taker_of(slot), "grp": plane},
            device_id_type=MESH,
        )

    def each_sent(action):
        def one(slot):
            @pl.when(idle_side(slot, upper) == jnp.where(live, 0, 1))
            def _():
                action(slot)

        each_slot(one)

    def send(slot):
        out[slot] = row_scaled(nb[wanted[taker_of(slot)]].astype(jnp.float32)).astype(jnp.bfloat16)
        fetch_copy(slot).start()

    each_sent(send)

    def rows_of(t):
        return pl.ds(pl.multiple_of(t * CHUNK_ROWS, CHUNK_ROWS), CHUNK_ROWS)

    def back_copy(t, slot):
        idle = idle_side(slot, upper)
        return pltpu.make_async_remote_copy(
            src_ref=back.at[slot, rows_of(t)],
            dst_ref=returned.at[t, crossed(slot, idle)],
            send_sem=back_send.at[t, slot],
            recv_sem=back_recv.at[t, crossed(slot, idle)],
            device_id={"rows": owner_of(slot), "grp": owner_plane(slot)},
            device_id_type=MESH,
        )

    def back_arrival(t, slot):
        return pltpu.make_async_remote_copy(
            src_ref=back.at[slot, rows_of(t)],
            dst_ref=returned.at[t, slot],
            send_sem=back_send.at[t, slot],
            recv_sem=back_recv.at[t, slot],
            device_id={"rows": lister_of(slot), "grp": owner_plane(slot)},
            device_id_type=MESH,
        )

    def one_hot(block_of):
        col = lax.broadcasted_iota(jnp.int32, (8, SLOTS * PIECE), 1)
        takes = jnp.zeros((8, SLOTS * PIECE), jnp.int32)
        for term in range(SLOTS):
            takes = jnp.where(col // PIECE == term, (block_of(term) + HALF * mine) % BLK_DEV, takes)
        row_id = lax.broadcasted_iota(jnp.int32, (BLK_DEV * PIECE, SLOTS * PIECE), 0)
        col_id = lax.broadcasted_iota(jnp.int32, (BLK_DEV * PIECE, SLOTS * PIECE), 1)
        return jnp.where(row_id == takes[0:1] * PIECE + col_id % PIECE, 1.0, 0.0).astype(jnp.bfloat16)

    @pl.when(live)
    def _():
        def normalise(b):
            nb[b] = row_scaled(nb[b].astype(jnp.float32)).astype(jnp.bfloat16)

        each(BLK_DEV, normalise)

        @pl.when(upper == 1)
        def _():
            fetched[0] = jnp.zeros((BLOCK, FEATURES), jnp.bfloat16)
            for t in range(CHUNKS):
                returned[t, 0] = jnp.zeros((CHUNK_ROWS, FEATURES), jnp.bfloat16)

        def diagonal(k):
            block = nb[mine * HALF + k]
            weight = cubed(nt_dot(block, block)).astype(jnp.bfloat16)
            totals[k] = jnp.dot(weight, block, preferred_element_type=jnp.float32)
            totals[HALF + k] = jnp.zeros((BLOCK, FEATURES), jnp.float32)

        each(HALF, diagonal)
        spread[SLOTS // ROUND] = one_hot(lambda term: wanted[lister_of(term)])
        for turn in range(SLOTS // ROUND):
            spread[turn] = one_hot(
                lambda term: links[owner_of(slot_at(turn * ROUND + term // LINKS)) * LINKS + term % LINKS]
            )
        link_col = lax.broadcasted_iota(jnp.int32, (BLOCK, LINKS * BLOCK), 1)

        def visit(turn, step):
            slot = slot_at(turn * ROUND + step)
            peer = owner_of(slot)

            @pl.when(not_self(slot))
            def _():
                fetch_copy(slot).wait_recv()

            for j in range(LINKS):
                cat[j * BLOCK:(j + 1) * BLOCK] = nb[links[peer * LINKS + j]]
            remote = fetched[slot]
            weight = jnp.where(
                link_col < counts[peer] * BLOCK, cubed(nt_dot(remote, cat[...])), 0.0
            ).astype(jnp.bfloat16)
            back[slot] = jnp.dot(weight, cat[...], preferred_element_type=jnp.float32).astype(jnp.bfloat16)

            @pl.when(not_self(slot))
            def _():
                back_copy(0, slot).start()

            forward[pl.ds(step * LINKS, LINKS)] = (
                tn_dot(weight, remote).astype(jnp.bfloat16).reshape(LINKS, BLOCK, FEATURES)
            )

        def work(turn):
            each(ROUND, lambda step: visit(turn, step))

            def piece(g):
                rows = pl.ds(pl.multiple_of(g * PIECE, PIECE), PIECE)
                terms = forward[:, rows, :].reshape(ROUND * LINKS * PIECE, FEATURES)
                sums = jnp.dot(spread[turn], terms, preferred_element_type=jnp.float32)
                totals[:, rows, :] += sums.reshape(BLK_DEV, PIECE, FEATURES)

            each(BLOCK // PIECE, piece)

        each(SLOTS // ROUND, work)
        for t in range(1, CHUNKS):
            each_slot(lambda slot: back_copy(t, slot).start())

    def along(src, dst, send, recv, t, side):
        return pltpu.make_async_remote_copy(
            src_ref=src, dst_ref=dst, send_sem=send.at[t], recv_sem=recv.at[t],
            device_id={"rows": me, "grp": side}, device_id_type=MESH,
        )

    def half_copy(t):
        return along(nb.at[pl.ds(0, HALF), rows_of(t)], half_in.at[:, rows_of(t)], half_send, half_recv, t, inner)

    def result(t):
        return nb.at[pl.ds(HALF, HALF), rows_of(t)]

    def out_half(t, which):
        return refined.at[pl.ds(which * HALF, HALF), rows_of(t)]

    def pair_copy(t):
        return along(result(t), out_half(t, mine), pair_send, pair_recv, t, inner)

    def next_copy(t):
        return along(result(t), out_half(t, mine), next_send, next_recv, t, outer)

    def near_copy(t):
        spot = refined.at[pl.ds((1 - mine) * HALF, NEAR), rows_of(t)]
        return along(spot, spot, near_send, near_recv, t, outer)

    def far_copy(t):
        spot = refined.at[pl.ds(mine * HALF + NEAR, HALF - NEAR), rows_of(t)]
        return along(spot, spot, far_send, far_recv, t, outer)

    def local_copy(t):
        return pltpu.make_async_copy(result(t), out_half(t, mine), local_sem.at[t])

    @pl.when(live)
    def _():
        def tick(t):
            @pl.when(t < CHUNKS)
            def _():
                each_slot(lambda slot: back_arrival(t, slot).wait_recv())

                def piece(g):
                    rows = pl.ds(pl.multiple_of(g * PIECE, PIECE), PIECE)
                    spot = pl.ds(pl.multiple_of(t * CHUNK_ROWS + g * PIECE, PIECE), PIECE)
                    came = returned[t, :, rows, :].reshape(SLOTS * PIECE, FEATURES)
                    sums = jnp.dot(spread[SLOTS // ROUND], came, preferred_element_type=jnp.float32)
                    sums = sums.reshape(BLK_DEV, PIECE, FEATURES)
                    totals[0:HALF, spot, :] += sums[0:HALF]
                    nb[0:HALF, spot, :] = (totals[HALF:BLK_DEV, spot, :] + sums[HALF:BLK_DEV]).astype(jnp.bfloat16)

                each(CHUNK_ROWS // PIECE, piece)
                half_copy(t).start()

            @pl.when(jnp.logical_and(t >= 1, t < CHUNKS + 1))
            def _():
                now = t - 1
                half_copy(now).wait_recv()

                def finish_block(k):
                    summed = totals[k, rows_of(now), :] + half_in[k, rows_of(now), :].astype(jnp.float32)
                    nb[HALF + k, rows_of(now), :] = row_scaled(summed).astype(jnp.bfloat16)

                each(HALF, finish_block)
                pair_copy(now).start()
                next_copy(now).start()
                local_copy(now).start()

            @pl.when(t >= 2)
            def _():
                pair_copy(t - 2).wait_recv()
                near_copy(t - 2).start()

        each(CHUNKS + 2, tick)

        def finish(t):
            half_copy(t).wait_send()
            pair_copy(t).wait_send()
            next_copy(t).wait_send()
            near_copy(t).wait_send()
            local_copy(t).wait()

        each(CHUNKS, finish)
        for t in range(CHUNKS):
            each_slot(lambda slot: back_copy(t, slot).wait_send())

    @pl.when(jnp.logical_not(live))
    def _():
        def tick(t):
            next_copy(t).wait_recv()
            far_copy(t).start()

        each(CHUNKS, tick)

        def finish(t):
            near_copy(t).wait_recv()
            far_copy(t).wait()

        each(CHUNKS, finish)

    each_sent(lambda slot: fetch_copy(slot).wait_send())


def on_device(embeddings, partner, links, counts):
    blocks = (BLK_DEV, BLOCK, FEATURES)
    smem = pl.BlockSpec(memory_space=pltpu.SMEM)
    dma = pltpu.SemaphoreType.DMA

    def vmem(*shape):
        return pltpu.VMEM(shape + (FEATURES,), jnp.bfloat16)

    refined = pl.pallas_call(
        whole_kernel,
        out_shape=jax.ShapeDtypeStruct(blocks, jnp.bfloat16),
        in_specs=[smem, smem, smem, pl.BlockSpec(memory_space=pl.ANY)],
        out_specs=pl.BlockSpec(memory_space=pl.ANY),
        scratch_shapes=[
            vmem(BLK_DEV, BLOCK),
            vmem(SLOTS, BLOCK),
            vmem(SLOTS, BLOCK),
            vmem(LINKS * BLOCK),
            vmem(ROUND * LINKS, BLOCK),
            pltpu.VMEM(blocks, jnp.float32),
            vmem(SLOTS, BLOCK),
            pltpu.VMEM((SLOTS // ROUND + 1, BLK_DEV * PIECE, SLOTS * PIECE), jnp.bfloat16),
            vmem(CHUNKS, SLOTS, CHUNK_ROWS),
            vmem(HALF, BLOCK),
            dma((BLK_DEV,)),
            dma((SLOTS,)),
            dma((SLOTS,)),
            dma((CHUNKS, SLOTS)),
            dma((CHUNKS, SLOTS)),
        ] + [dma((CHUNKS,))] * 11,
        compiler_params=pltpu.CompilerParams(
            collective_id=0, has_side_effects=True, vmem_limit_bytes=62 * 2**20
        ),
        name="whole",
    )(partner.reshape(-1), links.reshape(-1), counts.reshape(-1), embeddings.reshape(blocks))
    return refined.reshape(BLK_DEV * BLOCK, FEATURES)


def solution(mesh):
    placed = (P("rows", None), P(None, "rows"), P("rows", None, None), P("rows", None))
    return jax.shard_map(
        on_device, mesh=mesh, in_specs=placed, out_specs=P("rows", None), check_vma=False
    )
```

time: 864 us -> 179 us (0.21)
  waiting for transfers between devices: 386 us -> 0 us
  blocking collectives: 173 us -> 0 us
  Pallas kernels: 0 us -> 170 us
  other arithmetic: 144 us -> 0 us
  local copies, waits for them, and re-layouts: 68.5 us -> 7.27 us
  matrix products: 48 us -> 0 us
  loops' own time: 18.6 us -> 0 us
  between operations: 13.5 us -> 0.01 us
    psum x1 -> x0, waiting for transfers between devices: 228 us -> none  [on_device(): summed = lax.psum(totals, 'grp')]
    all_to_all x1 -> x0, blocking collectives: 173 us -> none  [on_device(): lax.all_to_all(returned, 'rows', split_axis=0, concat_axis=0, tiled=True)]
    pallas_call x0 -> x1, Pallas kernels: none -> 170 us  [on_device(): pl.pallas_call(whole_kernel, out_shape=jax.ShapeDtypeStruct(blocks, jnp.b...]
    all_to_all x1 -> x0, waiting for transfers between devices: 159 us -> none  [on_device(): lax.all_to_all(outgoing, 'rows', split_axis=0, concat_axis=0, tiled=True)]
    scatter-add x8 -> x0, other arithmetic: 103 us -> none  [the longest x1 56.5 us: on_device(): totals = totals.at[wanted].add(came_back.astype(jnp.float32))]
    dot_general x22 -> x0, matrix products: 48 us -> none  [the longest x7 20.6 us: visit(): jnp.einsum('kab,kad->bd', pair_weight, own_blocks, preferred_element_type...]
    gather x10 -> x0, local copies, waits for them, and re-layouts: 34.9 us -> none  [the longest x7 24 us: visit(): own_blocks = blocks[picked]]
    convert_element_type x3 -> x0, other arithmetic: 24.3 us -> none  [the longest x1 9.02 us: on_device(): totals = totals.at[wanted].add(came_back.astype(jnp.float32))]
  transfers between devices with their start and end apart: 2 -> 0, of which waited for: 2 -> 0; matrix products, arithmetic and copies ran while one was open for 2% -> 0% of each run, Pallas kernels for 0% -> 0%
where the time goes in v3:
time: 179 us; the launch traced here: 178 us
  Pallas kernels  170 us (95%)
  local copies, waits for them, and re-layouts  7.27 us (4%)
    pallas_call x1, Pallas kernels, on_device(): pl.pallas_call(whole_kernel, out_shape=jax.ShapeDtypeStruct(blocks, jnp.b...  170 us
    unnamed x2, local copies, waits for them, and re-layouts  6.65 us

profile of v3, /device:TPU:14, one launch (start us, length us, event | category | flops | bytes accessed | tf_op | source)
XLA Modules:
  0.0 177.7 jit_solution(16278378858519121057)
XLA Ops:
  0.0 0.8 copy.6
  0.8 0.6 reshape.16.links
  1.4 170.4 %whole.1 = bf16[16,256,768]{2,1,0:T(8,128)(2,1)} custom-call(s32[32]{0:T(128)} %bitcast.6, s32[128]{0:T(128)} %reshape.16.links, s32[32]{0:T(128)} %bitcast.7, bf16[16,256,768]{2,1,0:T(8,128)(2,1)} %bitcast.5), custom_call_target="tpu_custom_call" | custom-call | tf_op jit(solution)/shard_map/whole/pallas_call | solution.py:371
  171.8 5.9 %copy.8 = bf16[4096,768]{1,0:T(8,128)(2,1)} copy(bf16[4096,768]{1,0:T(8,128)(2,1)} %bitcast.4) | data formatting | bytes 12582912

commit v4 on v3

--- a/solution.py
+++ b/solution.py
@@ -12,9 +12,11 @@
 LINKS = 4
 PLANES = 4
 SLOTS = 16
-ROUND = 4
-CHUNKS = 4
+CHUNKS = 8
 CHUNK_ROWS = BLOCK // CHUNKS
+BACKS = 4
+BACK_ROWS = BLOCK // BACKS
+WIDER = CHUNKS // BACKS
 PIECE = 16
 NEAR = 6
 MESH = pl.DeviceIdType.MESH
@@ -59,7 +61,8 @@
     return lax.dot_general(left, right, (((0,), (0,)), ((), ())), preferred_element_type=jnp.float32)
 
 
-def whole_kernel(wanted, links, counts, emb, refined, nb, out, fetched, cat, forward, totals, back, spread, returned,
+def whole_kernel(wanted, links, counts, emb, refined, nb, out, fetched, cat, kept, forward, totals, back, spread,
+                 back_spread, returned,
                  half_in, in_sem, fetch_send, fetch_recv, back_send, back_recv, half_send, half_recv, pair_send,
                  pair_recv, next_send, next_recv, near_send, near_recv, far_send, far_recv, local_sem):
     me = lax.axis_index("rows")
@@ -164,10 +167,13 @@
     def rows_of(t):
         return pl.ds(pl.multiple_of(t * CHUNK_ROWS, CHUNK_ROWS), CHUNK_ROWS)
 
+    def back_rows(t):
+        return pl.ds(pl.multiple_of(t * BACK_ROWS, BACK_ROWS), BACK_ROWS)
+
     def back_copy(t, slot):
         idle = idle_side(slot, upper)
         return pltpu.make_async_remote_copy(
-            src_ref=back.at[slot, rows_of(t)],
+            src_ref=back.at[slot, back_rows(t)],
             dst_ref=returned.at[t, crossed(slot, idle)],
             send_sem=back_send.at[t, slot],
             recv_sem=back_recv.at[t, crossed(slot, idle)],
@@ -177,7 +183,7 @@
 
     def back_arrival(t, slot):
         return pltpu.make_async_remote_copy(
-            src_ref=back.at[slot, rows_of(t)],
+            src_ref=back.at[slot, back_rows(t)],
             dst_ref=returned.at[t, slot],
             send_sem=back_send.at[t, slot],
             recv_sem=back_recv.at[t, slot],
@@ -185,13 +191,13 @@
             device_id_type=MESH,
         )
 
-    def one_hot(block_of):
-        col = lax.broadcasted_iota(jnp.int32, (8, SLOTS * PIECE), 1)
-        takes = jnp.zeros((8, SLOTS * PIECE), jnp.int32)
-        for term in range(SLOTS):
+    def one_hot(block_of, count):
+        col = lax.broadcasted_iota(jnp.int32, (8, count * PIECE), 1)
+        takes = jnp.zeros((8, count * PIECE), jnp.int32)
+        for term in range(count):
             takes = jnp.where(col // PIECE == term, (block_of(term) + HALF * mine) % BLK_DEV, takes)
-        row_id = lax.broadcasted_iota(jnp.int32, (BLK_DEV * PIECE, SLOTS * PIECE), 0)
-        col_id = lax.broadcasted_iota(jnp.int32, (BLK_DEV * PIECE, SLOTS * PIECE), 1)
+        row_id = lax.broadcasted_iota(jnp.int32, (BLK_DEV * PIECE, count * PIECE), 0)
+        col_id = lax.broadcasted_iota(jnp.int32, (BLK_DEV * PIECE, count * PIECE), 1)
         return jnp.where(row_id == takes[0:1] * PIECE + col_id % PIECE, 1.0, 0.0).astype(jnp.bfloat16)
 
     @pl.when(live)
@@ -204,25 +210,21 @@
         @pl.when(upper == 1)
         def _():
             fetched[0] = jnp.zeros((BLOCK, FEATURES), jnp.bfloat16)
-            for t in range(CHUNKS):
-                returned[t, 0] = jnp.zeros((CHUNK_ROWS, FEATURES), jnp.bfloat16)
+            for t in range(BACKS):
+                returned[t, 0] = jnp.zeros((BACK_ROWS, FEATURES), jnp.bfloat16)
 
         def diagonal(k):
             block = nb[mine * HALF + k]
             weight = cubed(nt_dot(block, block)).astype(jnp.bfloat16)
             totals[k] = jnp.dot(weight, block, preferred_element_type=jnp.float32)
-            totals[HALF + k] = jnp.zeros((BLOCK, FEATURES), jnp.float32)
 
         each(HALF, diagonal)
-        spread[SLOTS // ROUND] = one_hot(lambda term: wanted[lister_of(term)])
-        for turn in range(SLOTS // ROUND):
-            spread[turn] = one_hot(
-                lambda term: links[owner_of(slot_at(turn * ROUND + term // LINKS)) * LINKS + term % LINKS]
-            )
+        back_spread[...] = one_hot(lambda term: wanted[lister_of(term)], SLOTS)
+        spread[...] = one_hot(lambda term: links[owner_of(term // LINKS) * LINKS + term % LINKS], SLOTS * LINKS)
         link_col = lax.broadcasted_iota(jnp.int32, (BLOCK, LINKS * BLOCK), 1)
 
-        def visit(turn, step):
-            slot = slot_at(turn * ROUND + step)
+        def visit(turn):
+            slot = slot_at(turn)
             peer = owner_of(slot)
 
             @pl.when(not_self(slot))
@@ -231,9 +233,8 @@
 
             for j in range(LINKS):
                 cat[j * BLOCK:(j + 1) * BLOCK] = nb[links[peer * LINKS + j]]
-            remote = fetched[slot]
             weight = jnp.where(
-                link_col < counts[peer] * BLOCK, cubed(nt_dot(remote, cat[...])), 0.0
+                link_col < counts[peer] * BLOCK, cubed(nt_dot(fetched[slot], cat[...])), 0.0
             ).astype(jnp.bfloat16)
             back[slot] = jnp.dot(weight, cat[...], preferred_element_type=jnp.float32).astype(jnp.bfloat16)
 
@@ -241,23 +242,10 @@
             def _():
                 back_copy(0, slot).start()
 
-            forward[pl.ds(step * LINKS, LINKS)] = (
-                tn_dot(weight, remote).astype(jnp.bfloat16).reshape(LINKS, BLOCK, FEATURES)
-            )
-
-        def work(turn):
-            each(ROUND, lambda step: visit(turn, step))
-
-            def piece(g):
-                rows = pl.ds(pl.multiple_of(g * PIECE, PIECE), PIECE)
-                terms = forward[:, rows, :].reshape(ROUND * LINKS * PIECE, FEATURES)
-                sums = jnp.dot(spread[turn], terms, preferred_element_type=jnp.float32)
-                totals[:, rows, :] += sums.reshape(BLK_DEV, PIECE, FEATURES)
-
-            each(BLOCK // PIECE, piece)
-
-        each(SLOTS // ROUND, work)
-        for t in range(1, CHUNKS):
+            kept[slot] = weight.T.reshape(LINKS, BLOCK, BLOCK)
+
+        each(SLOTS, visit)
+        for t in range(1, BACKS):
             each_slot(lambda slot: back_copy(t, slot).start())
 
     def along(src, dst, send, recv, t, side):
@@ -297,16 +285,31 @@
         def tick(t):
             @pl.when(t < CHUNKS)
             def _():
-                each_slot(lambda slot: back_arrival(t, slot).wait_recv())
+                def ahead(slot):
+                    weight = kept[slot, :, rows_of(t), :].reshape(LINKS * CHUNK_ROWS, BLOCK)
+                    sums = jnp.dot(weight, fetched[slot], preferred_element_type=jnp.float32)
+                    forward[pl.ds(slot * LINKS, LINKS)] = (
+                        sums.astype(jnp.bfloat16).reshape(LINKS, CHUNK_ROWS, FEATURES)
+                    )
+
+                each(SLOTS, ahead)
+
+                @pl.when(t % WIDER == 0)
+                def _():
+                    each_slot(lambda slot: back_arrival(t // WIDER, slot).wait_recv())
 
                 def piece(g):
                     rows = pl.ds(pl.multiple_of(g * PIECE, PIECE), PIECE)
                     spot = pl.ds(pl.multiple_of(t * CHUNK_ROWS + g * PIECE, PIECE), PIECE)
-                    came = returned[t, :, rows, :].reshape(SLOTS * PIECE, FEATURES)
-                    sums = jnp.dot(spread[SLOTS // ROUND], came, preferred_element_type=jnp.float32)
+                    back_spot = pl.ds(pl.multiple_of((t % WIDER) * CHUNK_ROWS + g * PIECE, PIECE), PIECE)
+                    terms = forward[:, rows, :].reshape(SLOTS * LINKS * PIECE, FEATURES)
+                    came = returned[t // WIDER, :, back_spot, :].reshape(SLOTS * PIECE, FEATURES)
+                    sums = jnp.dot(spread[...], terms, preferred_element_type=jnp.float32) + jnp.dot(
+                        back_spread[...], came, preferred_element_type=jnp.float32
+                    )
                     sums = sums.reshape(BLK_DEV, PIECE, FEATURES)
-                    totals[0:HALF, spot, :] += sums[0:HALF]
-                    nb[0:HALF, spot, :] = (totals[HALF:BLK_DEV, spot, :] + sums[HALF:BLK_DEV]).astype(jnp.bfloat16)
+                    totals[:, spot, :] += sums[0:HALF]
+                    nb[0:HALF, spot, :] = sums[HALF:BLK_DEV].astype(jnp.bfloat16)
 
                 each(CHUNK_ROWS // PIECE, piece)
                 half_copy(t).start()
@@ -340,7 +343,7 @@
             local_copy(t).wait()
 
         each(CHUNKS, finish)
-        for t in range(CHUNKS):
+        for t in range(BACKS):
             each_slot(lambda slot: back_copy(t, slot).wait_send())
 
     @pl.when(jnp.logical_not(live))
@@ -378,17 +381,19 @@
             vmem(SLOTS, BLOCK),
             vmem(SLOTS, BLOCK),
             vmem(LINKS * BLOCK),
-            vmem(ROUND * LINKS, BLOCK),
-            pltpu.VMEM(blocks, jnp.float32),
+            pltpu.VMEM((SLOTS, LINKS, BLOCK, BLOCK), jnp.bfloat16),
+            vmem(SLOTS * LINKS, CHUNK_ROWS),
+            pltpu.VMEM((HALF, BLOCK, FEATURES), jnp.float32),
             vmem(SLOTS, BLOCK),
-            pltpu.VMEM((SLOTS // ROUND + 1, BLK_DEV * PIECE, SLOTS * PIECE), jnp.bfloat16),
-            vmem(CHUNKS, SLOTS, CHUNK_ROWS),
+            pltpu.VMEM((BLK_DEV * PIECE, SLOTS * LINKS * PIECE), jnp.bfloat16),
+            pltpu.VMEM((BLK_DEV * PIECE, SLOTS * PIECE), jnp.bfloat16),
+            vmem(BACKS, SLOTS, BACK_ROWS),
             vmem(HALF, BLOCK),
             dma((BLK_DEV,)),
             dma((SLOTS,)),
             dma((SLOTS,)),
-            dma((CHUNKS, SLOTS)),
-            dma((CHUNKS, SLOTS)),
+            dma((BACKS, SLOTS)),
+            dma((BACKS, SLOTS)),
         ] + [dma((CHUNKS,))] * 11,
         compiler_params=pltpu.CompilerParams(
             collective_id=0, has_side_effects=True, vmem_limit_bytes=62 * 2**20

time: 179 us -> 167 us (0.933)
  the two profiles are of different devices: /device:TPU:14 before, /device:TPU:7 now
where the time goes in v4:
time: 167 us; the launch traced here: 166 us
  Pallas kernels  159 us (95%)
  local copies, waits for them, and re-layouts  7.27 us (4%)
    pallas_call x1, Pallas kernels, on_device(): pl.pallas_call(whole_kernel, out_shape=jax.ShapeDtypeStruct(blocks, jnp.b...  159 us
    unnamed x2, local copies, waits for them, and re-layouts  6.65 us

profile of v4, /device:TPU:7, one launch (start us, length us, event | category | flops | bytes accessed | tf_op | source)
XLA Modules:
  0.0 166.5 jit_solution(918478098042094640)
XLA Ops:
  0.0 0.8 copy.6
  0.8 0.6 reshape.16.links
  1.4 159.2 %whole.1 = bf16[16,256,768]{2,1,0:T(8,128)(2,1)} custom-call(s32[32]{0:T(128)} %bitcast.6, s32[128]{0:T(128)} %reshape.16.links, s32[32]{0:T(128)} %bitcast.7, bf16[16,256,768]{2,1,0:T(8,128)(2,1)} %bitcast.5), custom_call_target="tpu_custom_call" | custom-call | tf_op jit(solution)/shard_map/whole/pallas_call | solution.py:374
  160.6 5.9 %copy.8 = bf16[4096,768]{1,0:T(8,128)(2,1)} copy(bf16[4096,768]{1,0:T(8,128)(2,1)} %bitcast.4) | data formatting | bytes 12582912

commit v5 on v4

--- a/solution.py
+++ b/solution.py
@@ -18,7 +18,6 @@
 BACK_ROWS = BLOCK // BACKS
 WIDER = CHUNKS // BACKS
 PIECE = 16
-NEAR = 6
 MESH = pl.DeviceIdType.MESH
 
 
@@ -64,7 +63,7 @@
 def whole_kernel(wanted, links, counts, emb, refined, nb, out, fetched, cat, kept, forward, totals, back, spread,
                  back_spread, returned,
                  half_in, in_sem, fetch_send, fetch_recv, back_send, back_recv, half_send, half_recv, pair_send,
-                 pair_recv, next_send, next_recv, near_send, near_recv, far_send, far_recv, local_sem):
+                 pair_recv, next_send, next_recv, near_send, near_recv, local_sem):
     me = lax.axis_index("rows")
     plane = lax.axis_index("grp")
     x, y, core = me // 8, (me // 2) % 4, me % 2
@@ -220,7 +219,7 @@
 
         each(HALF, diagonal)
         back_spread[...] = one_hot(lambda term: wanted[lister_of(term)], SLOTS)
-        spread[...] = one_hot(lambda term: links[owner_of(term // LINKS) * LINKS + term % LINKS], SLOTS * LINKS)
+        spread[...] = one_hot(lambda term: links[term % LINKS, owner_of(term // LINKS)], SLOTS * LINKS)
         link_col = lax.broadcasted_iota(jnp.int32, (BLOCK, LINKS * BLOCK), 1)
 
         def visit(turn):
@@ -232,7 +231,7 @@
                 fetch_copy(slot).wait_recv()
 
             for j in range(LINKS):
-                cat[j * BLOCK:(j + 1) * BLOCK] = nb[links[peer * LINKS + j]]
+                cat[j * BLOCK:(j + 1) * BLOCK] = nb[links[j, peer]]
             weight = jnp.where(
                 link_col < counts[peer] * BLOCK, cubed(nt_dot(fetched[slot], cat[...])), 0.0
             ).astype(jnp.bfloat16)
@@ -270,12 +269,8 @@
         return along(result(t), out_half(t, mine), next_send, next_recv, t, outer)
 
     def near_copy(t):
-        spot = refined.at[pl.ds((1 - mine) * HALF, NEAR), rows_of(t)]
+        spot = out_half(t, 1 - mine)
         return along(spot, spot, near_send, near_recv, t, outer)
-
-    def far_copy(t):
-        spot = refined.at[pl.ds(mine * HALF + NEAR, HALF - NEAR), rows_of(t)]
-        return along(spot, spot, far_send, far_recv, t, outer)
 
     def local_copy(t):
         return pltpu.make_async_copy(result(t), out_half(t, mine), local_sem.at[t])
@@ -350,13 +345,11 @@
     def _():
         def tick(t):
             next_copy(t).wait_recv()
-            far_copy(t).start()
 
         each(CHUNKS, tick)
 
         def finish(t):
             near_copy(t).wait_recv()
-            far_copy(t).wait()
 
         each(CHUNKS, finish)
 
@@ -394,12 +387,12 @@
             dma((SLOTS,)),
             dma((BACKS, SLOTS)),
             dma((BACKS, SLOTS)),
-        ] + [dma((CHUNKS,))] * 11,
+        ] + [dma((CHUNKS,))] * 9,
         compiler_params=pltpu.CompilerParams(
             collective_id=0, has_side_effects=True, vmem_limit_bytes=62 * 2**20
         ),
         name="whole",
-    )(partner.reshape(-1), links.reshape(-1), counts.reshape(-1), embeddings.reshape(blocks))
+    )(partner.reshape(-1), links[0].T, counts.reshape(-1), embeddings.reshape(blocks))
     return refined.reshape(BLK_DEV * BLOCK, FEATURES)
 
 

time: 167 us -> 161 us (0.964)
  the two profiles are of different devices: /device:TPU:7 before, /device:TPU:26 now
where the time goes in v5:
time: 161 us
  Pallas kernels  155 us (96%)
  local copies, waits for them, and re-layouts  5.89 us (4%)
    pallas_call x1, Pallas kernels, on_device(): pl.pallas_call(whole_kernel, out_shape=jax.ShapeDtypeStruct(blocks, jnp.b...  155 us
    unnamed x1, local copies, waits for them, and re-layouts  5.89 us

profile of v5, /device:TPU:26, one launch (start us, length us, event | category | flops | bytes accessed | tf_op | source)
XLA Modules:
  0.0 161.2 jit_solution(11983606709528582993)
XLA Ops:
  0.0 155.3 %whole.1 = bf16[16,256,768]{2,1,0:T(8,128)(2,1)} custom-call(s32[32]{0:T(128)} %bitcast.10, s32[4,32]{1,0:T(4,128)} %bitcast.9, s32[32]{0:T(128)} %bitcast.11, bf16[16,256,768]{2,1,0:T(8,128)(2,1)} %bitcast.8), custom_call_target="tpu_custom_call" | custom-call | tf_op jit(solution)/shard_map/whole/pallas_call | solution.py:367
  155.3 5.9 %copy.6 = bf16[4096,768]{1,0:T(8,128)(2,1)} copy(bf16[4096,768]{1,0:T(8,128)(2,1)} %bitcast.7) | data formatting | bytes 12582912

commit v6 on v5

--- a/solution.py
+++ b/solution.py
@@ -244,8 +244,14 @@
             kept[slot] = weight.T.reshape(LINKS, BLOCK, BLOCK)
 
         each(SLOTS, visit)
+        def send_rest(t, slot, idle):
+            @pl.when(idle_side(slot, upper) == idle)
+            def _():
+                back_copy(t, slot).start()
+
         for t in range(1, BACKS):
-            each_slot(lambda slot: back_copy(t, slot).start())
+            for idle in (1, 0):
+                each_slot(lambda slot: send_rest(t, slot, idle))
 
     def along(src, dst, send, recv, t, side):
         return pltpu.make_async_remote_copy(

time: 161 us -> 160 us (level)
  the two profiles are of different devices: /device:TPU:26 before, /device:TPU:14 now
where the time goes in v6:
time: 160 us; the launch traced here: 159 us
  Pallas kernels  153 us (96%)
  local copies, waits for them, and re-layouts  5.89 us (4%)
    pallas_call x1, Pallas kernels, on_device(): pl.pallas_call(whole_kernel, out_shape=jax.ShapeDtypeStruct(blocks, jnp.b...  153 us
    unnamed x1, local copies, waits for them, and re-layouts  5.89 us

profile of v6, /device:TPU:14, one launch (start us, length us, event | category | flops | bytes accessed | tf_op | source)
XLA Modules:
  0.0 158.6 jit_solution(10495526315083586162)
XLA Ops:
  0.0 152.7 %whole.1 = bf16[16,256,768]{2,1,0:T(8,128)(2,1)} custom-call(s32[32]{0:T(128)} %bitcast.10, s32[4,32]{1,0:T(4,128)} %bitcast.9, s32[32]{0:T(128)} %bitcast.11, bf16[16,256,768]{2,1,0:T(8,128)(2,1)} %bitcast.8), custom_call_target="tpu_custom_call" | custom-call | tf_op jit(solution)/shard_map/whole/pallas_call | solution.py:373
  152.7 5.9 %copy.6 = bf16[4096,768]{1,0:T(8,128)(2,1)} copy(bf16[4096,768]{1,0:T(8,128)(2,1)} %bitcast.7) | data formatting | bytes 12582912

commit v7 on v6

--- a/solution.py
+++ b/solution.py
@@ -283,18 +283,19 @@
 
     @pl.when(live)
     def _():
+        def forward_sums(t):
+            def one(slot):
+                weight = kept[slot, :, rows_of(t), :].reshape(LINKS * CHUNK_ROWS, BLOCK)
+                sums = jnp.dot(weight, fetched[slot], preferred_element_type=jnp.float32)
+                forward[pl.ds(slot * LINKS, LINKS)] = sums.astype(jnp.bfloat16).reshape(LINKS, CHUNK_ROWS, FEATURES)
+
+            each(SLOTS, one)
+
+        forward_sums(0)
+
         def tick(t):
             @pl.when(t < CHUNKS)
             def _():
-                def ahead(slot):
-                    weight = kept[slot, :, rows_of(t), :].reshape(LINKS * CHUNK_ROWS, BLOCK)
-                    sums = jnp.dot(weight, fetched[slot], preferred_element_type=jnp.float32)
-                    forward[pl.ds(slot * LINKS, LINKS)] = (
-                        sums.astype(jnp.bfloat16).reshape(LINKS, CHUNK_ROWS, FEATURES)
-                    )
-
-                each(SLOTS, ahead)
-
                 @pl.when(t % WIDER == 0)
                 def _():
                     each_slot(lambda slot: back_arrival(t // WIDER, slot).wait_recv())
@@ -334,6 +335,10 @@
                 pair_copy(t - 2).wait_recv()
                 near_copy(t - 2).start()
 
+            @pl.when(t + 1 < CHUNKS)
+            def _():
+                forward_sums(t + 1)
+
         each(CHUNKS + 2, tick)
 
         def finish(t):
@@ -372,7 +377,7 @@
 
     refined = pl.pallas_call(
         whole_kernel,
-        out_shape=jax.ShapeDtypeStruct(blocks, jnp.bfloat16),
+        out_shape=pltpu.VMEM(blocks, jnp.bfloat16),
         in_specs=[smem, smem, smem, pl.BlockSpec(memory_space=pl.ANY)],
         out_specs=pl.BlockSpec(memory_space=pl.ANY),
         scratch_shapes=[
@@ -395,7 +400,7 @@
             dma((BACKS, SLOTS)),
         ] + [dma((CHUNKS,))] * 9,
         compiler_params=pltpu.CompilerParams(
-            collective_id=0, has_side_effects=True, vmem_limit_bytes=62 * 2**20
+            collective_id=0, has_side_effects=True, vmem_limit_bytes=56 * 2**20
         ),
         name="whole",
     )(partner.reshape(-1), links[0].T, counts.reshape(-1), embeddings.reshape(blocks))

time: 160 us -> 156 us (0.975)
  local copies, waits for them, and re-layouts: 5.89 us -> 2.71 us
    unnamed x1, local copies, waits for them, and re-layouts: 5.89 us -> 2.71 us
where the time goes in v7:
time: 156 us; the launch traced here: 155 us
  Pallas kernels  153 us (98%)
  local copies, waits for them, and re-layouts  2.71 us (2%)
    pallas_call x1, Pallas kernels, on_device(): pl.pallas_call(whole_kernel, out_shape=pltpu.VMEM(blocks, jnp.bfloat16),...  153 us

profile of v7, /device:TPU:14, one launch (start us, length us, event | category | flops | bytes accessed | tf_op | source)
XLA Modules:
  0.0 155.3 jit_solution(12220248792244716419)
XLA Ops:
  0.0 152.6 %whole.1 = bf16[16,256,768]{2,1,0:T(8,128)(2,1)S(1)} custom-call(s32[32]{0:T(128)} %bitcast.10, s32[4,32]{1,0:T(4,128)} %bitcast.9, s32[32]{0:T(128)} %bitcast.11, bf16[16,256,768]{2,1,0:T(8,128)(2,1)} %bitcast.8), custom_call_target="tpu_custom_call" | custom-call | tf_op jit(solution)/shard_map/whole/pallas_call | solution.py:378
  152.6 2.7 %copy.6 = bf16[4096,768]{1,0:T(8,128)(2,1)} copy(bf16[4096,768]{1,0:T(8,128)(2,1)S(1)} %bitcast.7) | data formatting | bytes 12582912

commit v8 on v7

--- a/solution.py
+++ b/solution.py
@@ -63,7 +63,7 @@
 def whole_kernel(wanted, links, counts, emb, refined, nb, out, fetched, cat, kept, forward, totals, back, spread,
                  back_spread, returned,
                  half_in, in_sem, fetch_send, fetch_recv, back_send, back_recv, half_send, half_recv, pair_send,
-                 pair_recv, next_send, next_recv, near_send, near_recv, local_sem):
+                 pair_recv, next_send, next_recv, near_send, near_recv):
     me = lax.axis_index("rows")
     plane = lax.axis_index("grp")
     x, y, core = me // 8, (me // 2) % 4, me % 2
@@ -262,24 +262,18 @@
     def half_copy(t):
         return along(nb.at[pl.ds(0, HALF), rows_of(t)], half_in.at[:, rows_of(t)], half_send, half_recv, t, inner)
 
-    def result(t):
-        return nb.at[pl.ds(HALF, HALF), rows_of(t)]
-
     def out_half(t, which):
         return refined.at[pl.ds(which * HALF, HALF), rows_of(t)]
 
     def pair_copy(t):
-        return along(result(t), out_half(t, mine), pair_send, pair_recv, t, inner)
+        return along(out_half(t, mine), out_half(t, mine), pair_send, pair_recv, t, inner)
 
     def next_copy(t):
-        return along(result(t), out_half(t, mine), next_send, next_recv, t, outer)
+        return along(out_half(t, mine), out_half(t, mine), next_send, next_recv, t, outer)
 
     def near_copy(t):
         spot = out_half(t, 1 - mine)
         return along(spot, spot, near_send, near_recv, t, outer)
-
-    def local_copy(t):
-        return pltpu.make_async_copy(result(t), out_half(t, mine), local_sem.at[t])
 
     @pl.when(live)
     def _():
@@ -323,12 +317,11 @@
 
                 def finish_block(k):
                     summed = totals[k, rows_of(now), :] + half_in[k, rows_of(now), :].astype(jnp.float32)
-                    nb[HALF + k, rows_of(now), :] = row_scaled(summed).astype(jnp.bfloat16)
+                    refined[mine * HALF + k, rows_of(now), :] = row_scaled(summed).astype(jnp.bfloat16)
 
                 each(HALF, finish_block)
                 pair_copy(now).start()
                 next_copy(now).start()
-                local_copy(now).start()
 
             @pl.when(t >= 2)
             def _():
@@ -346,7 +339,6 @@
             pair_copy(t).wait_send()
             next_copy(t).wait_send()
             near_copy(t).wait_send()
-            local_copy(t).wait()
 
         each(CHUNKS, finish)
         for t in range(BACKS):
@@ -379,7 +371,7 @@
         whole_kernel,
         out_shape=pltpu.VMEM(blocks, jnp.bfloat16),
         in_specs=[smem, smem, smem, pl.BlockSpec(memory_space=pl.ANY)],
-        out_specs=pl.BlockSpec(memory_space=pl.ANY),
+        out_specs=pl.BlockSpec(memory_space=pltpu.VMEM),
         scratch_shapes=[
             vmem(BLK_DEV, BLOCK),
             vmem(SLOTS, BLOCK),
@@ -398,7 +390,7 @@
             dma((SLOTS,)),
             dma((BACKS, SLOTS)),
             dma((BACKS, SLOTS)),
-        ] + [dma((CHUNKS,))] * 9,
+        ] + [dma((CHUNKS,))] * 8,
         compiler_params=pltpu.CompilerParams(
             collective_id=0, has_side_effects=True, vmem_limit_bytes=56 * 2**20
         ),

time: 156 us -> 156 us (level)
  no operation moved by 1% of the time
where the time goes in v8:
time: 156 us; the launch traced here: 155 us
  Pallas kernels  152 us (97%)
  local copies, waits for them, and re-layouts  2.71 us (2%)
    pallas_call x1, Pallas kernels, on_device(): pl.pallas_call(whole_kernel, out_shape=pltpu.VMEM(blocks, jnp.bfloat16),...  152 us

profile of v8, /device:TPU:14, one launch (start us, length us, event | category | flops | bytes accessed | tf_op | source)
XLA Modules:
  0.0 155.1 jit_solution(2856546117511358708)
XLA Ops:
  0.0 152.4 %whole.1 = bf16[16,256,768]{2,1,0:T(8,128)(2,1)S(1)} custom-call(s32[32]{0:T(128)} %bitcast.10, s32[4,32]{1,0:T(4,128)} %bitcast.9, s32[32]{0:T(128)} %bitcast.11, bf16[16,256,768]{2,1,0:T(8,128)(2,1)} %bitcast.8), custom_call_target="tpu_custom_call" | custom-call | tf_op jit(solution)/shard_map/whole/pallas_call | solution.py:370
  152.4 2.7 %copy.6 = bf16[4096,768]{1,0:T(8,128)(2,1)} copy(bf16[4096,768]{1,0:T(8,128)(2,1)S(1)} %bitcast.7) | data formatting | bytes 12582912
